TPU v7x, 256 devices: a whole 4x4x8 slice. The times are simulated.
256 devices in a mesh: section: 4 (over z_hi), seq: 64 (over z_lo, x, y, core).
Axes of the slice: x: 4, y: 4, z: 8 (z_hi: 4, z_lo: 2; z = z_hi * 2 + z_lo), core: 2. Of those that a mesh axis runs over, the one named last changes fastest.
Arguments:
- video_saved: bfloat16 [4, 2, 4096, 1536], P('section', None, 'seq'), may hold values from -30 to 30
- audio_saved: bfloat16 [4, 2, 2048, 1536], P('section', None, 'seq'), may hold values from -6 to 6
- video_cotangent: bfloat16 [2, 4096, 1536], P(None, 'seq'), may hold values from -6 to 6
- audio_cotangent: bfloat16 [2, 2048, 1536], P(None, 'seq'), may hold values from -6 to 6
- modulation: float32 [4, 4, 1536], P('section'), may hold values from 0.25 to 1.75
- video_window: int32 [64, 2], P('seq'), may hold values from 0 to 256, as said below
- audio_window: int32 [64, 2], P('seq'), may hold values from 0 to 256, as said below
Outputs:
- video_grad: bfloat16 [4, 2, 4096, 1536], P('section', None, 'seq')
- audio_grad: bfloat16 [4, 2, 2048, 1536], P('section', None, 'seq')
- modulation_grad: float32 [4, 4, 1536], P('section')
Inputs may be any that keep to these rules, and one draw needn't show every extreme that they name: `video_window`: row i: the window of shard i in audio blocks; it holds blocks 4i - 1 to 4i + 4 clipped to the sequence and lies within 4i - 2 to 4i + 6 clipped to the sequence; some shard's window spans that whole range. `audio_window`: row i: the window of shard i in video blocks, with the same bounds.
All inputs are finite; a program needn't handle non-finite values.
Results may differ from a plain program's by a relative error of at most 0.012.
Values may be sent and summed in bfloat16 or wider, within the bound.
No kernel may reach another device: no remote copies, remote signals or barrier semaphores. Data moves between devices by JAX's collectives and lax.ppermute only.
A program may use at most 128 MiB of HBM per device.

v0:
```python
import jax
import jax.numpy as jnp
from jax import lax
from jax.sharding import PartitionSpec as P

HDIM = 128


precise = lax.Precision.HIGHEST


def passed_along(value, axis, steps):
    count = lax.axis_size(axis)
    first, last = (max(0, -steps), min(count, count - steps))
    return lax.ppermute(value, axis, [(source, source + steps) for source in range(first, last)])


def padded(cells, sides, width):
    for axis, dim in sides:
        count = lax.axis_size(axis)
        ends = count - 1
        head = lax.slice_in_dim(cells, 0, width, axis=dim)
        tail = lax.slice_in_dim(cells, cells.shape[dim] - width, cells.shape[dim], axis=dim)
        cells = jnp.concatenate(
            [
                lax.ppermute(tail, axis, [(i, (i + 1) % count) for i in range(ends)]),
                cells,
                lax.ppermute(head, axis, [((i + 1) % count, i) for i in range(ends)]),
            ],
            axis=dim,
        )
    return cells


def window_mask(shard, shard_rows, block_rows, window):
    positions = shard * shard_rows - shard_rows // 2 + jnp.arange(2 * shard_rows, dtype=jnp.int32)
    blocks = jnp.floor_divide(positions, block_rows)
    return (blocks >= window[0]) & (blocks < window[1])


def cross_attend(queries, keys, values, allowed, head_size):
    count = queries.shape[0]
    width = queries.shape[1]
    heads = width // head_size
    query_heads = queries.reshape(count, heads, head_size)
    key_heads = keys.reshape(keys.shape[0], heads, head_size)
    value_heads = values.reshape(values.shape[0], heads, head_size)
    scores = jnp.einsum("qhd,khd->hqk", query_heads, key_heads, precision=precise) * head_size ** (
        -0.5
    )
    scores = jnp.where(allowed[None, None, :], scores, -1e30)
    largest = lax.stop_gradient(jnp.max(scores, axis=2, keepdims=True))
    weights = jnp.exp(scores - largest)
    weights = weights / jnp.sum(weights, axis=2, keepdims=True)
    mixed = jnp.einsum("hqk,khd->qhd", weights, value_heads, precision=precise)
    return mixed.reshape(count, width)


def block_layer(video_ext, audio_ext, mods, video_allowed, audio_allowed, head_size):
    video_count = video_ext.shape[0] // 2
    audio_count = audio_ext.shape[0] // 2
    video_own = video_ext[video_count // 2 : video_count // 2 + video_count]
    audio_own = audio_ext[audio_count // 2 : audio_count // 2 + audio_count]
    video_mixed = cross_attend(video_own, audio_ext * mods[0], audio_ext, video_allowed, head_size)
    audio_mixed = cross_attend(audio_own, video_ext * mods[1], video_ext, audio_allowed, head_size)
    return (video_own + mods[2] * video_mixed, audio_own + mods[3] * audio_mixed)


def local(
    video_saved,
    audio_saved,
    video_cotangent,
    audio_cotangent,
    modulation,
    video_window,
    audio_window,
):
    sections = lax.axis_size("section")
    micros = video_saved.shape[1]
    video_count = video_saved.shape[2]
    audio_count = audio_saved.shape[2]
    width = video_saved.shape[3]
    video_half = video_count // 2
    audio_half = audio_count // 2
    section_index = lax.axis_index("section")
    shard = lax.axis_index("seq")
    mods = modulation[0]
    video_allowed = window_mask(shard, audio_count, audio_count // 4, video_window[0])
    audio_allowed = window_mask(shard, video_count, video_count // 4, audio_window[0])
    video_out = video_saved[0] * 0
    audio_out = audio_saved[0] * 0
    mod_total = jnp.zeros((4, width), jnp.float32)
    is_top = section_index == sections - 1
    video_sent = video_cotangent[0]
    audio_sent = audio_cotangent[0]

    def local_layer(video_ext, audio_ext, layer_mods):
        return block_layer(video_ext, audio_ext, layer_mods, video_allowed, audio_allowed, HDIM)

    for tick in range(micros + sections - 1):
        micro = tick - (sections - 1 - section_index)
        valid = (micro >= 0) & (micro < micros)
        picked = jnp.clip(micro, 0, micros - 1)
        video_now = lax.dynamic_index_in_dim(video_saved[0], picked, 0, keepdims=False)
        audio_now = lax.dynamic_index_in_dim(audio_saved[0], picked, 0, keepdims=False)
        video_top = lax.dynamic_index_in_dim(video_cotangent, picked, 0, keepdims=False)
        audio_top = lax.dynamic_index_in_dim(audio_cotangent, picked, 0, keepdims=False)
        if tick > 0:
            video_recv, audio_recv = passed_along((video_sent, audio_sent), "section", -1)
            video_down = jnp.where(is_top, video_top, video_recv)
            audio_down = jnp.where(is_top, audio_top, audio_recv)
        else:
            video_down = video_top
            audio_down = audio_top
        video_ext = padded(video_now, (("seq", 0),), video_half)
        audio_ext = padded(audio_now, (("seq", 0),), audio_half)
        _, pull = jax.vjp(
            local_layer, video_ext.astype(jnp.float32), audio_ext.astype(jnp.float32), mods
        )
        video_part, audio_part, mod_part = pull(
            (video_down.astype(jnp.float32), audio_down.astype(jnp.float32))
        )
        video_from_above, audio_from_above = passed_along(
            (video_part[:video_half], audio_part[:audio_half]), "seq", -1
        )
        video_from_below, audio_from_below = passed_along(
            (video_part[video_half + video_count :], audio_part[audio_half + audio_count :]),
            "seq",
            1,
        )
        video_total = video_part[video_half : video_half + video_count] + jnp.concatenate(
            [video_from_below, video_from_above], axis=0
        )
        audio_total = audio_part[audio_half : audio_half + audio_count] + jnp.concatenate(
            [audio_from_below, audio_from_above], axis=0
        )
        video_sent = video_total.astype(jnp.bfloat16)
        audio_sent = audio_total.astype(jnp.bfloat16)
        video_out = jnp.where(
            valid, lax.dynamic_update_index_in_dim(video_out, video_sent, picked, 0), video_out
        )
        audio_out = jnp.where(
            valid, lax.dynamic_update_index_in_dim(audio_out, audio_sent, picked, 0), audio_out
        )
        mod_total = mod_total + jnp.where(valid, mod_part, 0.0)
    mod_summed = lax.psum(mod_total, "seq")
    return (video_out[None], audio_out[None], mod_summed[None])


def solution(mesh):
    return jax.shard_map(
        local,
        mesh=mesh,
        in_specs=(
            P("section", None, "seq", None),
            P("section", None, "seq", None),
            P(None, "seq", None),
            P(None, "seq", None),
            P("section", None, None),
            P("seq", None),
            P("seq", None),
        ),
        out_specs=(
            P("section", None, "seq", None),
            P("section", None, "seq", None),
            P("section", None, None),
        ),
        check_vma=False,
    )
```

profile of v0, /device:TPU:32, one launch (start us, length us, event | category | flops | bytes accessed | tf_op | source)
XLA Modules:
  0.0 692.4 jit_solution(10335484768806992210)
XLA Ops:
  4.6 7.9 %collective-permute-start.3 = (bf16[16,1536]{1,0:T(8,128)(2,1)}, bf16[16,1536]{1,0:T(8,128)(2,1)}, u32[]{:S(2)}, u32[]{:S(2)}) collective-permute-start(bf16[16,1536]{1,0:T(8,128)(2,1)} %get-tuple-element.90), channel_id=1, source_target_pairs={{1,0},{2,1},{3,2},{4,3},{5,4},{6,5},{7,6},{8,7},{9,8},{10,9},{11,1... | collective-permute-start | bytes 147464 | tf_op jit(solution)/shard_map/ppermute | solution.py:28
  15.4 7.9 %collective-permute-start.1 = (bf16[32,1536]{1,0:T(8,128)(2,1)}, bf16[32,1536]{1,0:T(8,128)(2,1)}, u32[]{:S(2)}, u32[]{:S(2)}) collective-permute-start(bf16[32,1536]{1,0:T(8,128)(2,1)} %get-tuple-element.67), channel_id=1, source_target_pairs={{1,0},{2,1},{3,2},{4,3},{5,4},{6,5},{7,6},{8,7},{9,8},{10,9},{11,1... | collective-permute-start | bytes 294920 | tf_op jit(solution)/shard_map/ppermute | solution.py:28
  43.4 7.8 %collective-permute-start.13 = (bf16[16,1536]{1,0:T(8,128)(2,1)S(1)}, bf16[16,1536]{1,0:T(8,128)(2,1)S(1)}, u32[]{:S(2)}, u32[]{:S(2)}) collective-permute-start(bf16[16,1536]{1,0:T(8,128)(2,1)S(1)} %copy-done.145), channel_id=1, source_target_pairs={{1,0},{2,1},{3,2},{4,3},{5,4},{6,5},{7,6},{8,7},{9,8},{10,9},{11,1... | collective-permute-start | bytes 147464 | tf_op jit(solution)/shard_map/ppermute | solution.py:28
  60.3 8.0 %collective-permute-start.10 = (bf16[32,1536]{1,0:T(8,128)(2,1)}, bf16[32,1536]{1,0:T(8,128)(2,1)}, u32[]{:S(2)}, u32[]{:S(2)}) collective-permute-start(bf16[32,1536]{1,0:T(8,128)(2,1)} %get-tuple-element.65), channel_id=1, source_target_pairs={{1,0},{2,1},{3,2},{4,3},{5,4},{6,5},{7,6},{8,7},{9,8},{10,9},{11,1... | collective-permute-start | bytes 294920 | tf_op jit(solution)/shard_map/ppermute | solution.py:28
  73.1 6.4 collective-permute-done.22
  87.7 5.1 collective-permute-done.32
  92.8 2.8 collective-permute-start.33
  101.8 5.2 collective-permute-done.42
  107.0 2.7 collective-permute-start.43
  116.1 7.9 %collective-permute-start.20 = (bf16[32,1536]{1,0:T(8,128)(2,1)}, bf16[32,1536]{1,0:T(8,128)(2,1)}, u32[]{:S(2)}, u32[]{:S(2)}) collective-permute-start(bf16[32,1536]{1,0:T(8,128)(2,1)} %get-tuple-element.63), channel_id=1, source_target_pairs={{1,0},{2,1},{3,2},{4,3},{5,4},{6,5},{7,6},{8,7},{9,8},{10,9},{11,1... | collective-permute-start | bytes 294920 | tf_op jit(solution)/shard_map/ppermute | solution.py:28
  140.3 7.8 %collective-permute-start.30 = (bf16[32,1536]{1,0:T(8,128)(2,1)S(1)}, bf16[32,1536]{1,0:T(8,128)(2,1)S(1)}, u32[]{:S(2)}, u32[]{:S(2)}) collective-permute-start(bf16[32,1536]{1,0:T(8,128)(2,1)S(1)} %copy-done.127), channel_id=1, source_target_pairs={{1,0},{2,1},{3,2},{4,3},{5,4},{6,5},{7,6},{8,7},{9,8},{10,9},{11,1... | collective-permute-start | bytes 294920 | tf_op jit(solution)/shard_map/ppermute | solution.py:28
  153.8 7.8 %collective-permute-start.40 = (bf16[32,1536]{1,0:T(8,128)(2,1)S(1)}, bf16[32,1536]{1,0:T(8,128)(2,1)S(1)}, u32[]{:S(2)}, u32[]{:S(2)}) collective-permute-start(bf16[32,1536]{1,0:T(8,128)(2,1)S(1)} %copy-done.125), channel_id=1, source_target_pairs={{1,0},{2,1},{3,2},{4,3},{5,4},{6,5},{7,6},{8,7},{9,8},{10,9},{11,1... | collective-permute-start | bytes 294920 | tf_op jit(solution)/shard_map/ppermute | solution.py:28
  168.8 2.4 collective-permute-start.4
  172.7 7.5 %collective-permute-start.7 = (f32[16,1536]{1,0:T(8,128)S(1)}, f32[16,1536]{1,0:T(8,128)S(1)}, u32[]{:S(2)}, u32[]{:S(2)}) collective-permute-start(f32[16,1536]{1,0:T(8,128)S(1)} %get-tuple-element.79), channel_id=1, source_target_pairs={{1,0},{2,1},{3,2},{4,3},{5,4},{6,5},{7,6},{8,7},{9,8},{10,9},{11,1... | collective-permute-start | bytes 294920 | tf_op jit(solution)/shard_map/ppermute | solution.py:15
  196.9 4.2 collective-permute-done.8
  209.7 2.5 fusion.15
  223.4 5.9 collective-permute-start.15
  231.4 7.9 %collective-permute-start.17 = (f32[16,1536]{1,0:T(8,128)S(1)}, f32[16,1536]{1,0:T(8,128)S(1)}, u32[]{:S(2)}, u32[]{:S(2)}) collective-permute-start(f32[16,1536]{1,0:T(8,128)S(1)} %get-tuple-element.77), channel_id=1, source_target_pairs={{1,0},{2,1},{3,2},{4,3},{5,4},{6,5},{7,6},{8,7},{9,8},{10,9},{11,1... | collective-permute-start | bytes 294920 | tf_op jit(solution)/shard_map/ppermute | solution.py:15
  242.5 6.9 collective-permute-done.16
  253.2 4.9 collective-permute-done.18
  267.2 2.5 fusion.16
  285.5 7.4 %collective-permute-start.27 = (f32[16,1536]{1,0:T(8,128)S(1)}, f32[16,1536]{1,0:T(8,128)S(1)}, u32[]{:S(2)}, u32[]{:S(2)}) collective-permute-start(f32[16,1536]{1,0:T(8,128)S(1)} %get-tuple-element.75), channel_id=1, source_target_pairs={{1,0},{2,1},{3,2},{4,3},{5,4},{6,5},{7,6},{8,7},{9,8},{10,9},{11,1... | collective-permute-start | bytes 294920 | tf_op jit(solution)/shard_map/ppermute | solution.py:15
  297.1 5.9 collective-permute-done.26
  306.8 6.2 collective-permute-done.28
  322.1 2.5 fusion.17
  340.1 8.0 %collective-permute-done.34 = f32[32,1536]{1,0:T(8,128)S(1)} collective-permute-done((f32[32,1536]{1,0:T(8,128)S(1)}, f32[32,1536]{1,0:T(8,128)S(1)}, u32[]{:S(2)}, u32[]{:S(2)}) %collective-permute-start.34) | collective-permute-done | bytes 196640 | tf_op jit(solution)/shard_map/ppermute | solution.py:15
  352.4 5.7 collective-permute-done.41
  369.8 5.3 collective-permute-done.36
  378.7 5.0 collective-permute-done.38
  395.8 2.4 collective-permute-start.44
  398.6 7.5 %collective-permute-start.47 = (f32[16,1536]{1,0:T(8,128)S(1)}, f32[16,1536]{1,0:T(8,128)S(1)}, u32[]{:S(2)}, u32[]{:S(2)}) collective-permute-start(f32[16,1536]{1,0:T(8,128)S(1)} %get-tuple-element.56), channel_id=1, source_target_pairs={{1,0},{2,1},{3,2},{4,3},{5,4},{6,5},{7,6},{8,7},{9,8},{10,9},{11,1... | collective-permute-start | bytes 294920 | tf_op jit(solution)/shard_map/ppermute | solution.py:15
  408.4 281.5 %psum.7 = f32[1,4,1536]{2,1,0:T(4,128)} all-reduce(f32[1,4,1536]{2,1,0:T(4,128)S(1)} %add_bitcast_fusion), channel_id=1, replica_groups=mesh['section'=4,'seq'=64] {'seq'}, use_global_device_ids=true, to_apply=%region_50.51 | all-reduce | flops 6144 | bytes 49152 | tf_op jit(solution)/shard_map/psum | solution.py:146
  (736 shorter events, 228.3 us)
Async XLA Ops:
  2.7 40.1 %collective-permute-start.2 = (bf16[16,1536]{1,0:T(8,128)(2,1)}, bf16[16,1536]{1,0:T(8,128)(2,1)}, u32[]{:S(2)}, u32[]{:S(2)}) collective-permute-start(bf16[16,1536]{1,0:T(8,128)(2,1)} %get-tuple-element.91), channel_id=1, source_target_pairs={{0,1},{1,2},{2,3},{3,4},{4,5},{5,6},{6,7},{7,8},{8,9},{9,10},{10,1... | collective-permute-start | bytes 147464 | tf_op jit(solution)/shard_map/ppermute | solution.py:26
  4.6 47.5 %collective-permute-start.3 = (bf16[16,1536]{1,0:T(8,128)(2,1)}, bf16[16,1536]{1,0:T(8,128)(2,1)}, u32[]{:S(2)}, u32[]{:S(2)}) collective-permute-start(bf16[16,1536]{1,0:T(8,128)(2,1)} %get-tuple-element.90), channel_id=1, source_target_pairs={{1,0},{2,1},{3,2},{4,3},{5,4},{6,5},{7,6},{8,7},{9,8},{10,9},{11,1... | collective-permute-start | bytes 147464 | tf_op jit(solution)/shard_map/ppermute | solution.py:28
  13.4 102.7 %collective-permute-start = (bf16[32,1536]{1,0:T(8,128)(2,1)}, bf16[32,1536]{1,0:T(8,128)(2,1)}, u32[]{:S(2)}, u32[]{:S(2)}) collective-permute-start(bf16[32,1536]{1,0:T(8,128)(2,1)} %get-tuple-element.68), channel_id=1, source_target_pairs={{0,1},{1,2},{2,3},{3,4},{4,5},{5,6},{6,7},{7,8},{8,9},{9,10},{10,1... | collective-permute-start | bytes 294920 | tf_op jit(solution)/shard_map/ppermute | solution.py:26
  15.4 109.7 %collective-permute-start.1 = (bf16[32,1536]{1,0:T(8,128)(2,1)}, bf16[32,1536]{1,0:T(8,128)(2,1)}, u32[]{:S(2)}, u32[]{:S(2)}) collective-permute-start(bf16[32,1536]{1,0:T(8,128)(2,1)} %get-tuple-element.67), channel_id=1, source_target_pairs={{1,0},{2,1},{3,2},{4,3},{5,4},{6,5},{7,6},{8,7},{9,8},{10,9},{11,1... | collective-permute-start | bytes 294920 | tf_op jit(solution)/shard_map/ppermute | solution.py:28
  23.2 37.1 %collective-permute-start.12 = (bf16[16,1536]{1,0:T(8,128)(2,1)}, bf16[16,1536]{1,0:T(8,128)(2,1)}, u32[]{:S(2)}, u32[]{:S(2)}) collective-permute-start(bf16[16,1536]{1,0:T(8,128)(2,1)} %get-tuple-element.89), channel_id=1, source_target_pairs={{0,1},{1,2},{2,3},{3,4},{4,5},{5,6},{6,7},{7,8},{8,9},{9,10},{10,1... | collective-permute-start | bytes 147464 | tf_op jit(solution)/shard_map/ppermute | solution.py:26
  43.4 25.8 %collective-permute-start.13 = (bf16[16,1536]{1,0:T(8,128)(2,1)S(1)}, bf16[16,1536]{1,0:T(8,128)(2,1)S(1)}, u32[]{:S(2)}, u32[]{:S(2)}) collective-permute-start(bf16[16,1536]{1,0:T(8,128)(2,1)S(1)} %copy-done.145), channel_id=1, source_target_pairs={{1,0},{2,1},{3,2},{4,3},{5,4},{6,5},{7,6},{8,7},{9,8},{10,9},{11,1... | collective-permute-start | bytes 147464 | tf_op jit(solution)/shard_map/ppermute | solution.py:28
  52.1 87.3 %collective-permute-start.9 = (bf16[32,1536]{1,0:T(8,128)(2,1)}, bf16[32,1536]{1,0:T(8,128)(2,1)}, u32[]{:S(2)}, u32[]{:S(2)}) collective-permute-start(bf16[32,1536]{1,0:T(8,128)(2,1)} %get-tuple-element.66), channel_id=1, source_target_pairs={{0,1},{1,2},{2,3},{3,4},{4,5},{5,6},{6,7},{7,8},{8,9},{9,10},{10,1... | collective-permute-start | bytes 294920 | tf_op jit(solution)/shard_map/ppermute | solution.py:26
  60.3 88.9 %collective-permute-start.10 = (bf16[32,1536]{1,0:T(8,128)(2,1)}, bf16[32,1536]{1,0:T(8,128)(2,1)}, u32[]{:S(2)}, u32[]{:S(2)}) collective-permute-start(bf16[32,1536]{1,0:T(8,128)(2,1)} %get-tuple-element.65), channel_id=1, source_target_pairs={{1,0},{2,1},{3,2},{4,3},{5,4},{6,5},{7,6},{8,7},{9,8},{10,9},{11,1... | collective-permute-start | bytes 294920 | tf_op jit(solution)/shard_map/ppermute | solution.py:28
  111.4 42.4 %collective-permute-start.19 = (bf16[32,1536]{1,0:T(8,128)(2,1)}, bf16[32,1536]{1,0:T(8,128)(2,1)}, u32[]{:S(2)}, u32[]{:S(2)}) collective-permute-start(bf16[32,1536]{1,0:T(8,128)(2,1)} %get-tuple-element.64), channel_id=1, source_target_pairs={{0,1},{1,2},{2,3},{3,4},{4,5},{5,6},{6,7},{7,8},{8,9},{9,10},{10,1... | collective-permute-start | bytes 294920 | tf_op jit(solution)/shard_map/ppermute | solution.py:26
  116.1 47.4 %collective-permute-start.20 = (bf16[32,1536]{1,0:T(8,128)(2,1)}, bf16[32,1536]{1,0:T(8,128)(2,1)}, u32[]{:S(2)}, u32[]{:S(2)}) collective-permute-start(bf16[32,1536]{1,0:T(8,128)(2,1)} %get-tuple-element.63), channel_id=1, source_target_pairs={{1,0},{2,1},{3,2},{4,3},{5,4},{6,5},{7,6},{8,7},{9,8},{10,9},{11,1... | collective-permute-start | bytes 294920 | tf_op jit(solution)/shard_map/ppermute | solution.py:28
  125.0 43.7 %collective-permute-start.29 = (bf16[32,1536]{1,0:T(8,128)(2,1)}, bf16[32,1536]{1,0:T(8,128)(2,1)}, u32[]{:S(2)}, u32[]{:S(2)}) collective-permute-start(bf16[32,1536]{1,0:T(8,128)(2,1)} %get-tuple-element.62), channel_id=1, source_target_pairs={{0,1},{1,2},{2,3},{3,4},{4,5},{5,6},{6,7},{7,8},{8,9},{9,10},{10,1... | collective-permute-start | bytes 294920 | tf_op jit(solution)/shard_map/ppermute | solution.py:26
  140.3 32.4 %collective-permute-start.30 = (bf16[32,1536]{1,0:T(8,128)(2,1)S(1)}, bf16[32,1536]{1,0:T(8,128)(2,1)S(1)}, u32[]{:S(2)}, u32[]{:S(2)}) collective-permute-start(bf16[32,1536]{1,0:T(8,128)(2,1)S(1)} %copy-done.127), channel_id=1, source_target_pairs={{1,0},{2,1},{3,2},{4,3},{5,4},{6,5},{7,6},{8,7},{9,8},{10,9},{11,1... | collective-permute-start | bytes 294920 | tf_op jit(solution)/shard_map/ppermute | solution.py:28
  150.0 33.2 %collective-permute-start.39 = (bf16[32,1536]{1,0:T(8,128)(2,1)S(1)}, bf16[32,1536]{1,0:T(8,128)(2,1)S(1)}, u32[]{:S(2)}, u32[]{:S(2)}) collective-permute-start(bf16[32,1536]{1,0:T(8,128)(2,1)S(1)} %copy-done.126), channel_id=1, source_target_pairs={{0,1},{1,2},{2,3},{3,4},{4,5},{5,6},{6,7},{7,8},{8,9},{9,10},{10,1... | collective-permute-start | bytes 294920 | tf_op jit(solution)/shard_map/ppermute | solution.py:26
  153.8 33.0 %collective-permute-start.40 = (bf16[32,1536]{1,0:T(8,128)(2,1)S(1)}, bf16[32,1536]{1,0:T(8,128)(2,1)S(1)}, u32[]{:S(2)}, u32[]{:S(2)}) collective-permute-start(bf16[32,1536]{1,0:T(8,128)(2,1)S(1)} %copy-done.125), channel_id=1, source_target_pairs={{1,0},{2,1},{3,2},{4,3},{5,4},{6,5},{7,6},{8,7},{9,8},{10,9},{11,1... | collective-permute-start | bytes 294920 | tf_op jit(solution)/shard_map/ppermute | solution.py:28
  163.6 31.1 %collective-permute-start.5 = (f32[32,1536]{1,0:T(8,128)S(1)}, f32[32,1536]{1,0:T(8,128)S(1)}, u32[]{:S(2)}, u32[]{:S(2)}) collective-permute-start(f32[32,1536]{1,0:T(8,128)S(1)} %get-tuple-element.54), channel_id=1, source_target_pairs={{1,0},{2,1},{3,2},{4,3},{5,4},{6,5},{7,6},{8,7},{9,8},{10,9},{11,1... | collective-permute-start | bytes 589832 | tf_op jit(solution)/shard_map/ppermute | solution.py:15
  168.8 25.9 %collective-permute-start.4 = (f32[32,1536]{1,0:T(8,128)S(1)}, f32[32,1536]{1,0:T(8,128)S(1)}, u32[]{:S(2)}, u32[]{:S(2)}) collective-permute-start(f32[32,1536]{1,0:T(8,128)S(1)} %get-tuple-element.53), channel_id=1, source_target_pairs={{0,1},{1,2},{2,3},{3,4},{4,5},{5,6},{6,7},{7,8},{8,9},{9,10},{10,1... | collective-permute-start | bytes 589832 | tf_op jit(solution)/shard_map/ppermute | solution.py:15
  172.7 19.3 %collective-permute-start.7 = (f32[16,1536]{1,0:T(8,128)S(1)}, f32[16,1536]{1,0:T(8,128)S(1)}, u32[]{:S(2)}, u32[]{:S(2)}) collective-permute-start(f32[16,1536]{1,0:T(8,128)S(1)} %get-tuple-element.79), channel_id=1, source_target_pairs={{1,0},{2,1},{3,2},{4,3},{5,4},{6,5},{7,6},{8,7},{9,8},{10,9},{11,1... | collective-permute-start | bytes 294920 | tf_op jit(solution)/shard_map/ppermute | solution.py:15
  195.5 19.7 %collective-permute-start.11 = (bf16[64,1536]{1,0:T(8,128)(2,1)}, bf16[64,1536]{1,0:T(8,128)(2,1)}, u32[]{:S(2)}, u32[]{:S(2)}) collective-permute-start(bf16[64,1536]{1,0:T(8,128)(2,1)} %get-tuple-element.44), channel_id=1, source_target_pairs={{64,0},{128,64},{192,128},{65,1},{129,65},{193,129},{66,2},{130,66... | collective-permute-start | bytes 589832 | tf_op jit(solution)/shard_map/ppermute | solution.py:15
  223.4 27.3 %collective-permute-start.15 = (f32[32,1536]{1,0:T(8,128)S(1)}, f32[32,1536]{1,0:T(8,128)S(1)}, u32[]{:S(2)}, u32[]{:S(2)}) collective-permute-start(f32[32,1536]{1,0:T(8,128)S(1)} %get-tuple-element.52), channel_id=1, source_target_pairs={{1,0},{2,1},{3,2},{4,3},{5,4},{6,5},{7,6},{8,7},{9,8},{10,9},{11,1... | collective-permute-start | bytes 589832 | tf_op jit(solution)/shard_map/ppermute | solution.py:15
  229.4 21.4 %collective-permute-start.14 = (f32[32,1536]{1,0:T(8,128)S(1)}, f32[32,1536]{1,0:T(8,128)S(1)}, u32[]{:S(2)}, u32[]{:S(2)}) collective-permute-start(f32[32,1536]{1,0:T(8,128)S(1)} %get-tuple-element.51), channel_id=1, source_target_pairs={{0,1},{1,2},{2,3},{3,4},{4,5},{5,6},{6,7},{7,8},{8,9},{9,10},{10,1... | collective-permute-start | bytes 589832 | tf_op jit(solution)/shard_map/ppermute | solution.py:15
  231.4 11.1 %collective-permute-start.17 = (f32[16,1536]{1,0:T(8,128)S(1)}, f32[16,1536]{1,0:T(8,128)S(1)}, u32[]{:S(2)}, u32[]{:S(2)}) collective-permute-start(f32[16,1536]{1,0:T(8,128)S(1)} %get-tuple-element.77), channel_id=1, source_target_pairs={{1,0},{2,1},{3,2},{4,3},{5,4},{6,5},{7,6},{8,7},{9,8},{10,9},{11,1... | collective-permute-start | bytes 294920 | tf_op jit(solution)/shard_map/ppermute | solution.py:15
  239.3 10.2 %collective-permute-start.16 = (f32[16,1536]{1,0:T(8,128)S(1)}, f32[16,1536]{1,0:T(8,128)S(1)}, u32[]{:S(2)}, u32[]{:S(2)}) collective-permute-start(f32[16,1536]{1,0:T(8,128)S(1)} %get-tuple-element.76), channel_id=1, source_target_pairs={{0,1},{1,2},{2,3},{3,4},{4,5},{5,6},{6,7},{7,8},{8,9},{9,10},{10,1... | collective-permute-start | bytes 294920 | tf_op jit(solution)/shard_map/ppermute | solution.py:15
  251.6 21.1 %collective-permute-start.21 = (bf16[64,1536]{1,0:T(8,128)(2,1)}, bf16[64,1536]{1,0:T(8,128)(2,1)}, u32[]{:S(2)}, u32[]{:S(2)}) collective-permute-start(bf16[64,1536]{1,0:T(8,128)(2,1)} %get-tuple-element.42), channel_id=1, source_target_pairs={{64,0},{128,64},{192,128},{65,1},{129,65},{193,129},{66,2},{130,66... | collective-permute-start | bytes 589832 | tf_op jit(solution)/shard_map/ppermute | solution.py:15
  280.9 23.5 %collective-permute-start.25 = (f32[32,1536]{1,0:T(8,128)S(1)}, f32[32,1536]{1,0:T(8,128)S(1)}, u32[]{:S(2)}, u32[]{:S(2)}) collective-permute-start(f32[32,1536]{1,0:T(8,128)S(1)} %get-tuple-element.50), channel_id=1, source_target_pairs={{1,0},{2,1},{3,2},{4,3},{5,4},{6,5},{7,6},{8,7},{9,8},{10,9},{11,1... | collective-permute-start | bytes 589832 | tf_op jit(solution)/shard_map/ppermute | solution.py:15
  283.0 21.4 %collective-permute-start.24 = (f32[32,1536]{1,0:T(8,128)S(1)}, f32[32,1536]{1,0:T(8,128)S(1)}, u32[]{:S(2)}, u32[]{:S(2)}) collective-permute-start(f32[32,1536]{1,0:T(8,128)S(1)} %get-tuple-element.49), channel_id=1, source_target_pairs={{0,1},{1,2},{2,3},{3,4},{4,5},{5,6},{6,7},{7,8},{8,9},{9,10},{10,1... | collective-permute-start | bytes 589832 | tf_op jit(solution)/shard_map/ppermute | solution.py:15
  285.5 11.6 %collective-permute-start.27 = (f32[16,1536]{1,0:T(8,128)S(1)}, f32[16,1536]{1,0:T(8,128)S(1)}, u32[]{:S(2)}, u32[]{:S(2)}) collective-permute-start(f32[16,1536]{1,0:T(8,128)S(1)} %get-tuple-element.75), channel_id=1, source_target_pairs={{1,0},{2,1},{3,2},{4,3},{5,4},{6,5},{7,6},{8,7},{9,8},{10,9},{11,1... | collective-permute-start | bytes 294920 | tf_op jit(solution)/shard_map/ppermute | solution.py:15
  305.2 22.4 %collective-permute-start.31 = (bf16[64,1536]{1,0:T(8,128)(2,1)}, bf16[64,1536]{1,0:T(8,128)(2,1)}, u32[]{:S(2)}, u32[]{:S(2)}) collective-permute-start(bf16[64,1536]{1,0:T(8,128)(2,1)} %get-tuple-element.40), channel_id=1, source_target_pairs={{64,0},{128,64},{192,128},{65,1},{129,65},{193,129},{66,2},{130,66... | collective-permute-start | bytes 589832 | tf_op jit(solution)/shard_map/ppermute | solution.py:15
  337.0 11.2 %collective-permute-start.34 = (f32[32,1536]{1,0:T(8,128)S(1)}, f32[32,1536]{1,0:T(8,128)S(1)}, u32[]{:S(2)}, u32[]{:S(2)}) collective-permute-start(f32[32,1536]{1,0:T(8,128)S(1)} %get-tuple-element.47), channel_id=1, source_target_pairs={{0,1},{1,2},{2,3},{3,4},{4,5},{5,6},{6,7},{7,8},{8,9},{9,10},{10,1... | collective-permute-start | bytes 589832 | tf_op jit(solution)/shard_map/ppermute | solution.py:15
  393.8 296.2 %collective-permute-start.45 = (f32[32,1536]{1,0:T(8,128)S(1)}, f32[32,1536]{1,0:T(8,128)}, u32[]{:S(2)}, u32[]{:S(2)}) collective-permute-start(f32[32,1536]{1,0:T(8,128)S(1)} %get-tuple-element.46), channel_id=1, source_target_pairs={{1,0},{2,1},{3,2},{4,3},{5,4},{6,5},{7,6},{8,7},{9,8},{10,9},{11,1... | collective-permute-start | bytes 589832 | tf_op jit(solution)/shard_map/ppermute | solution.py:15
  395.8 294.2 %collective-permute-start.44 = (f32[32,1536]{1,0:T(8,128)S(1)}, f32[32,1536]{1,0:T(8,128)}, u32[]{:S(2)}, u32[]{:S(2)}) collective-permute-start(f32[32,1536]{1,0:T(8,128)S(1)} %get-tuple-element.45), channel_id=1, source_target_pairs={{0,1},{1,2},{2,3},{3,4},{4,5},{5,6},{6,7},{7,8},{8,9},{9,10},{10,1... | collective-permute-start | bytes 589832 | tf_op jit(solution)/shard_map/ppermute | solution.py:15
  398.6 291.3 %collective-permute-start.47 = (f32[16,1536]{1,0:T(8,128)S(1)}, f32[16,1536]{1,0:T(8,128)S(1)}, u32[]{:S(2)}, u32[]{:S(2)}) collective-permute-start(f32[16,1536]{1,0:T(8,128)S(1)} %get-tuple-element.56), channel_id=1, source_target_pairs={{1,0},{2,1},{3,2},{4,3},{5,4},{6,5},{7,6},{8,7},{9,8},{10,9},{11,1... | collective-permute-start | bytes 294920 | tf_op jit(solution)/shard_map/ppermute | solution.py:15
  406.1 283.8 %collective-permute-start.46 = (f32[16,1536]{1,0:T(8,128)S(1)}, f32[16,1536]{1,0:T(8,128)S(1)}, u32[]{:S(2)}, u32[]{:S(2)}) collective-permute-start(f32[16,1536]{1,0:T(8,128)S(1)} %get-tuple-element.55), channel_id=1, source_target_pairs={{0,1},{1,2},{2,3},{3,4},{4,5},{5,6},{6,7},{7,8},{8,9},{9,10},{10,1... | collective-permute-start | bytes 294920 | tf_op jit(solution)/shard_map/ppermute | solution.py:15
  (230 other events, 1837.2 us)
where the time goes:
time: 705 us; the launch traced here: 692 us
  blocking collectives  281 us (40%)
  starting transfers between devices  162 us (23%)
  waiting for transfers between devices  72.7 us (10%)
  local copies, waits for them, and re-layouts  72 us (10%)
  matrix products  67.8 us (10%)
  other arithmetic  31.8 us (5%)
    psum x1, blocking collectives, local(): mod_summed = lax.psum(mod_total, 'seq')  281 us
    ppermute x28, starting transfers between devices, passed_along(): lax.ppermute(value, axis, [(source, source + steps) for source in range(f...  79.8 us
    ppermute x10, starting transfers between devices, padded(): lax.ppermute(head, axis, [((i + 1) % count, i) for i in range(ends)])  62.5 us
    ppermute x28, waiting for transfers between devices, passed_along(): lax.ppermute(value, axis, [(source, source + steps) for source in range(f...  54.8 us
    dot_general x30, matrix products, cross_attend(): mixed = jnp.einsum('hqk,khd->qhd', weights, value_heads, precision=precise)  36 us
    unnamed x452, local copies, waits for them, and re-layouts  35.2 us
    dot_general x30, matrix products, cross_attend(): jnp.einsum('qhd,khd->hqk', query_heads, key_heads, precision=precise)  31.8 us
    ppermute x10, starting transfers between devices, padded(): lax.ppermute(tail, axis, [(i, (i + 1) % count) for i in range(ends)])  19.6 us
  transfers between devices with their start and end apart: 48, of which 18 were waited for; matrix products, arithmetic and copies ran while one was open for 16% of the time, Pallas kernels for 0%

commit v1 on v0

v1 whole, which is shorter than its diff:
```python
import functools

import jax
import jax.numpy as jnp
from jax import lax
from jax.experimental import pallas as pl
from jax.experimental.pallas import tpu as pltpu
from jax.sharding import PartitionSpec as P


HDIM = 128
MB = 2
VH = 32
AH = 16
GROUP = VH + AH
HALF = MB * GROUP
ROWS = 2 * HALF
MODS = 16
SCALE = HDIM**-0.5
LARGE = 60
OWN_LIMIT = 40
F32 = jnp.float32
BF16 = jnp.bfloat16
SMEM = pl.BlockSpec(memory_space=pltpu.SMEM)


def call(body, out_shape, flops=0, moved=1 << 20, limit=40, **kw):
    return pl.pallas_call(
        body,
        out_shape=out_shape,
        cost_estimate=pl.CostEstimate(flops=flops, bytes_accessed=moved, transcendentals=0),
        compiler_params=pltpu.CompilerParams(vmem_limit_bytes=limit << 20),
        **kw,
    )


def shape(*dims, dtype=BF16):
    return jax.ShapeDtypeStruct(dims, dtype)


def dot(a, b, dims):
    return lax.dot_general(a, b, (dims, ((), ())), preferred_element_type=F32)


def rows_of(half, seq):
    odd = seq % 2
    part = odd if half == 0 else 1 - odd
    v_rows = pl.ds(pl.multiple_of(part * VH, VH), VH)
    a_rows = pl.ds(pl.multiple_of(part * AH, AH), AH)
    return v_rows, a_rows


def section_order(count):
    return sorted(range(count), key=lambda k: (k == 0, min(k, count - k)))


def prepare(order, *refs):
    half_refs = (len(refs) - 1 - len(order) - (0 in order)) // 2
    inputs, outs, fetched, sems = (
        refs[:half_refs],
        refs[half_refs : -1 - half_refs],
        refs[-1 - half_refs : -1],
        refs[-1],
    )
    copies = [
        pltpu.make_async_copy(source, target, sems.at[i])
        for i, (source, target) in enumerate(zip(inputs, fetched))
    ]
    for copy in copies:
        copy.start()
    for copy in copies:
        copy.wait()
    video, audio, mods, v_window, a_window = fetched[:5]
    count, width = lax.axis_size("section"), outs[0].shape[1]
    section, seq = lax.axis_index("section"), lax.axis_index("seq")
    ends = [v_window[0, 0], v_window[0, 1], a_window[0, 0], a_window[0, 1]]
    ends = [jnp.full((1, width), end - 4 * seq, jnp.int32).astype(F32) for end in ends]
    ends = jnp.concatenate(ends, axis=0).astype(BF16)
    for k, piece in zip(order, outs):
        columns = pl.ds(pl.multiple_of(lax.rem(section + k, count) * width, 128), width)
        for half in range(2):
            v_rows, a_rows = rows_of(half, seq)
            for m in range(MB):
                base = half * HALF + m * GROUP
                piece[base : base + VH] = video[0, m, v_rows, columns]
                piece[base + VH : base + GROUP] = audio[0, m, a_rows, columns]
                if k == 0:
                    video_cot, audio_cot = fetched[5:]
                    outs[-1][base : base + VH] = video_cot[m, v_rows, columns]
                    outs[-1][base + VH : base + GROUP] = audio_cot[m, a_rows, columns]
        value = mods[0, :, columns]
        high = value.astype(BF16)
        rest = value - high.astype(F32)
        middle = rest.astype(BF16)
        low = (rest - middle.astype(F32)).astype(BF16)
        piece[ROWS : ROWS + MODS] = jnp.concatenate([high, middle, low, ends], axis=0)


def assemble(*refs):
    pieces, (far, near, extra) = refs[:-3], refs[-3:]
    count, section = len(pieces), lax.axis_index("section")
    for k, piece in zip(section_order(count), pieces):
        layer = lax.rem(section - k + count, count)
        far[layer] = piece[:HALF]
        near[layer] = piece[HALF:ROWS]
        extra[layer] = piece[ROWS : ROWS + MODS]


def read_mods(extra):
    parts = extra[0].astype(F32)
    return parts[0:4] + parts[4:8] + parts[8:12]


def contexts(data, m):
    far_own, near_own, far_in, near_in = data
    at = m * GROUP
    refs = (far_in, far_own, near_own, near_in)
    video = [ref[0, at : at + VH] for ref in refs]
    audio = [ref[0, at + VH : at + GROUP] for ref in refs]
    return jnp.concatenate(video, axis=0), jnp.concatenate(audio, axis=0)


def allowed_row(extra, at, count):
    ends = extra[0].astype(F32)[:, :count].astype(jnp.int32)
    row = lax.broadcasted_iota(jnp.int32, (1, count), 1)
    per_piece = count // 4
    piece = row // per_piece
    piece = jnp.where(lax.axis_index("seq") % 2 == 1, 3 - piece, piece)
    block = 2 * piece - 2 + (row % per_piece) // (per_piece // 2)
    return (block >= ends[at : at + 1]) & (block < ends[at + 1 : at + 2])


def masks(extra):
    return allowed_row(extra, 12, 4 * AH), allowed_row(extra, 14, 4 * VH)


def split(value):
    high = value.astype(BF16)
    return high, (value - high.astype(F32)).astype(BF16)


def dot_rows(parts, b, dims):
    count = parts[0].shape[0]
    both = dot(jnp.concatenate(parts, axis=0), b, dims)
    return both[:count] + both[count:]


def softmax_all(units):
    scores = []
    for queries, context, allowed in units:
        products = dot_rows(split(queries), context, ((1,), (1,)))
        scores.append(jnp.where(allowed, products, -1e30))
    largest = [jnp.max(x, axis=1, keepdims=True) for x in scores]
    weights = [jnp.exp(x - y) for x, y in zip(scores, largest)]
    sums = [jnp.sum(x, axis=1, keepdims=True) for x in weights]
    return [x / y for x, y in zip(weights, sums)]


def heads_of(width):
    return [(h, slice(h * HDIM, (h + 1) * HDIM)) for h in range(width // HDIM)]


def forward_layer(data, extra, store):
    width = extra.shape[2]
    mods = read_mods(extra)
    v_allowed, a_allowed = masks(extra)
    v_scale = mods[0:1] * SCALE
    a_scale = mods[1:2] * SCALE
    keys, units = [], []
    for m in range(MB):
        v_ctx, a_ctx = contexts(data, m)
        v_own = v_ctx[VH : 3 * VH].astype(F32) * v_scale
        a_own = a_ctx[AH : 3 * AH].astype(F32) * a_scale
        for h, cols in heads_of(width):
            keys += [(0, m, h), (1, m, h)]
            units.append((v_own[:, cols], a_ctx[:, cols], v_allowed))
            units.append((a_own[:, cols], v_ctx[:, cols], a_allowed))
    for key, weights in zip(keys, softmax_all(units)):
        store(*key, weights)


def attend_back(units):
    grads = [split(cot * gate) for _, cot, _, _, _, gate in units]
    by_weights = [dot_rows(g, unit[3], ((1,), (1,))) for g, unit in zip(grads, units)]
    products = [unit[0] * by for by, unit in zip(by_weights, units)]
    means = [jnp.sum(product, axis=1, keepdims=True) for product in products]
    boths = [
        split(jnp.concatenate([unit[0], unit[0] * (by - mean)], axis=0))
        for by, mean, unit in zip(by_weights, means, units)
    ]
    outs = [dot_rows(both, unit[3], ((1,), (0,))) for both, unit in zip(boths, units)]
    found = []
    for grad, both, out, (_, cot, own, _, scale, _) in zip(grads, boths, outs, units):
        count = cot.shape[0]
        own32 = own.astype(F32)
        scaled = split(own32 * scale)
        high, low = (jnp.concatenate([g, q], axis=0) for g, q in zip(grad, scaled))
        by_context = dot(
            jnp.concatenate([both[0], both[1], both[0]], axis=0),
            jnp.concatenate([high, high, low], axis=0),
            ((0,), (0,)),
        )
        mixed, back = out[:count], out[count:]
        by_scale = jnp.sum(own32 * back, axis=0, keepdims=True) * SCALE
        by_gate = jnp.sum(cot * mixed, axis=0, keepdims=True)
        found.append((back * scale, by_context, by_scale, by_gate))
    return found


def backward_layer(data, extra, cots, load, outs):
    width = extra.shape[2]
    mods = read_mods(extra)
    own_out, far_out, near_out = outs
    units, places = [], []
    for m in range(MB):
        v_all, a_all = contexts(data, m)
        for h, cols in heads_of(width):
            v_ctx, a_ctx = v_all[:, cols], a_all[:, cols]
            first, second = m * GROUP, HALF + m * GROUP
            v_cot = jnp.concatenate(
                [cots[first : first + VH, cols], cots[second : second + VH, cols]], axis=0
            )
            a_cot = jnp.concatenate(
                [
                    cots[first + VH : first + GROUP, cols],
                    cots[second + VH : second + GROUP, cols],
                ],
                axis=0,
            )
            v_scale, a_scale = mods[0:1, cols] * SCALE, mods[1:2, cols] * SCALE
            v_own, a_own = v_ctx[VH : 3 * VH], a_ctx[AH : 3 * AH]
            units.append((load(0, m, h), v_cot, v_own, a_ctx, v_scale, mods[2:3, cols]))
            units.append((load(1, m, h), a_cot, a_own, v_ctx, a_scale, mods[3:4, cols]))
            places.append((h, cols, first, second))
    found = attend_back(units)
    by_mods = {}
    for at, (h, cols, first, second) in enumerate(places):
        v_q, a_by, s0, g2 = found[2 * at]
        a_q, v_by, s1, g3 = found[2 * at + 1]
        rows = jnp.concatenate([s0, s1, g2, g3], axis=0)
        by_mods[h] = by_mods[h] + rows if h in by_mods else rows
        v_total = units[2 * at][1] + v_q + v_by[VH : 3 * VH]
        a_total = units[2 * at + 1][1] + a_q + a_by[AH : 3 * AH]
        own_out[first : first + VH, cols] = v_total[:VH]
        own_out[first + VH : first + GROUP, cols] = a_total[:AH]
        own_out[second : second + VH, cols] = v_total[VH:]
        own_out[second + VH : second + GROUP, cols] = a_total[AH:]
        far_out[first : first + VH, cols] = v_by[:VH].astype(BF16)
        far_out[first + VH : first + GROUP, cols] = a_by[:AH].astype(BF16)
        near_out[first : first + VH, cols] = v_by[3 * VH :].astype(BF16)
        near_out[first + VH : first + GROUP, cols] = a_by[3 * AH :].astype(BF16)
    return jnp.concatenate([by_mods[h] for h, _ in heads_of(width)], axis=1)


def top_layer(far_own, near_own, far_in, near_in, extra, cots, own_out, far_out, near_out, mods):
    found = {}

    def store(*key_value):
        found[key_value[:3]] = key_value[3]

    data = (far_own, near_own, far_in, near_in)
    forward_layer(data, extra, store)
    mods[...] = jnp.zeros_like(mods)
    mods[mods.shape[0] - 1] = backward_layer(
        data, extra, cots[...].astype(F32), lambda *key: found[key], (own_out, far_out, near_out)
    )


def weights_ahead(far_own, near_own, far_in, near_in, extra, v_weights, a_weights):
    def store(kind, m, h, value):
        (v_weights, a_weights)[kind][0, m, h] = value

    forward_layer((far_own, near_own, far_in, near_in), extra, store)


def joined(own, far_in, near_in):
    first = own[:HALF].astype(F32) + far_in[...].astype(F32)
    second = own[HALF:].astype(F32) + near_in[...].astype(F32)
    return jnp.concatenate([first, second], axis=0).astype(BF16)


def lower_layer(layer, *refs):
    data, extra, (own, far_part, near_part, v_weights, a_weights, mods_in) = (
        refs[:4],
        refs[4],
        refs[5:11],
    )
    total_out, mods, *outs = refs[11:16]
    total = joined(own, far_part, near_part)
    total_out[...] = total
    mods[...] = mods_in[...]
    mods[layer] = backward_layer(
        data,
        extra,
        total.astype(F32),
        lambda kind, m, h: (v_weights, a_weights)[kind][0, m, h],
        outs,
    )
    for spread in refs[16:]:
        copies = spread.shape[0] // mods.shape[0]
        for at in range(spread.shape[0]):
            spread[at] = mods[at // copies]


def group_sum(own, moved):
    total = own[...] + moved[0][...]
    return total + (moved[1][...] + moved[2][...]) if len(moved) == 3 else total


def gather_totals(own, far_part, near_part, *refs):
    totals, spread, out, mods = refs[:-3], *refs[-3:]
    out[0] = joined(own, far_part, near_part)
    for at, total in enumerate(totals):
        out[at + 1] = total[...]
    count = out.shape[0]
    copies = spread.shape[0] // count
    chunks = []
    for c in range(count):
        chunks.append(sum((spread[c * copies + i] for i in range(1, copies)), spread[c * copies]))
    mods[0] = jnp.concatenate(chunks, axis=1)


def add_group(own, *refs):
    refs[-1][...] = group_sum(own, refs[:-1])


def finish(received, mods, *refs):
    moved, (video, audio, mods_out) = refs[:-3], refs[-3:]
    mods_out[...] = group_sum(mods, moved)
    count, _, width = received.shape
    seq = lax.axis_index("seq")
    for chunk in range(count):
        columns = pl.ds(chunk * width, width)
        for half in range(2):
            v_rows, a_rows = rows_of(half, seq)
            for m in range(MB):
                base = half * HALF + m * GROUP
                video[0, m, v_rows, columns] = received[chunk, base : base + VH]
                audio[0, m, a_rows, columns] = received[chunk, base + VH : base + GROUP]


def swap(value, first):
    pairs = [(i, i + 1) for i in range(first, lax.axis_size("seq") - 1, 2)]
    return lax.ppermute(value, "seq", pairs + [(b, a) for a, b in pairs])


def swap_near(value):
    return swap(value, 0)


def swap_far(value):
    return swap(value, 1)


def to_section(value, k):
    count = lax.axis_size("section")
    if k == 0:
        return value
    return lax.ppermute(value, "section", [(s, (s + k) % count) for s in range(count)])


def split_bits(count):
    return ((0, 5), ((1, 2), (3, 4))) if count == 64 else ((0,), ((1,),))


def home_and_sum(spread):
    sections, count = lax.axis_size("section"), lax.axis_size("seq")
    bits = split_bits(count)[0]
    mask = sum(1 << bit for bit in bits)
    members = [i for i in range(count) if i & ~mask == 0]
    groups = [
        [s * count + base + i for s in range(sections) for i in members]
        for base in range(count)
        if base & mask == 0
    ]
    return lax.all_to_all(
        spread, ("section", "seq"), 0, 0, axis_index_groups=groups, tiled=True
    )


def group_moves(value, bits):
    count = lax.axis_size("seq")
    masks = [1 << bits[0]]
    if len(bits) == 2:
        masks += [1 << bits[1], 1 << bits[0] | 1 << bits[1]]
    return [lax.ppermute(value, "seq", [(i, i ^ mask) for i in range(count)]) for mask in masks]


def local(video_saved, audio_saved, video_cot, audio_cot, modulation, v_window, a_window):
    sections, count = lax.axis_size("section"), lax.axis_size("seq")
    width = video_saved.shape[3] // sections
    heads = width // HDIM
    flops = 200_000_000

    def whole(*dims):
        return pl.BlockSpec(dims, lambda *_: (0,) * len(dims))

    def like(arrays):
        return [whole(*a.shape) for a in arrays]

    def run(body, arrays, outs, specs=None, **kw):
        return call(
            body,
            tuple(outs),
            grid=(1,),
            in_specs=specs or like(arrays),
            out_specs=tuple(like(outs)),
            **kw,
        )(*arrays)

    hbm = pl.BlockSpec(memory_space=pltpu.HBM)

    def run_prepare(order, arrays, outs, limit):
        return call(
            functools.partial(prepare, order),
            outs,
            grid=(1,),
            in_specs=[hbm] * len(arrays),
            out_specs=tuple(like(outs)),
            limit=limit,
            scratch_shapes=[
                (pltpu.VMEM if a.size > 2 else pltpu.SMEM)(a.shape, a.dtype) for a in arrays
            ]
            + [pltpu.SemaphoreType.DMA((len(arrays),))],
            name="prepare" if order[0] else "prepare_own",
        )(*arrays)

    inputs = (video_saved, audio_saved, modulation, v_window, a_window)
    piece = shape(ROWS + MODS, width)
    order = section_order(sections)
    sent = run_prepare(order[:-1], inputs, (piece,) * (sections - 1), LARGE)
    pieces = [to_section(value, k) for value, k in zip(sent, order)]
    own_piece, cots = run_prepare(
        order[-1:], inputs + (video_cot, audio_cot), (piece, shape(ROWS, width)), OWN_LIMIT
    )
    pieces.append(own_piece)
    far_own, near_own, extra = run(
        assemble,
        tuple(pieces),
        [shape(sections, HALF, width), shape(sections, HALF, width), shape(sections, MODS, width)],
        name="assemble",
    )
    far_in = swap_far(far_own)
    near_in = swap_near(near_own)
    data = (far_own, near_own, far_in, near_in, extra)

    def layer_specs(index):
        return [pl.BlockSpec((1,) + a.shape[1:], lambda *i: (index(*i), 0, 0)) for a in data]

    chain = [
        shape(ROWS, width, dtype=F32),
        shape(HALF, width),
        shape(HALF, width),
        shape(sections, 4, width, dtype=F32),
    ]
    top = sections - 1
    own, far_out, near_out, mods = run(
        top_layer,
        data + (cots,),
        chain,
        layer_specs(lambda *_: top) + like([cots]),
        flops=flops,
        name="top_layer",
    )
    blocks = [(1, MB, heads, 2 * VH, 4 * AH), (1, MB, heads, 2 * AH, 4 * VH)]
    weights = call(
        weights_ahead,
        tuple(shape(top, *block[1:], dtype=F32) for block in blocks),
        flops=3 * flops,
        grid=(top,),
        in_specs=layer_specs(lambda i: i),
        out_specs=tuple(pl.BlockSpec(block, lambda i: (i, 0, 0, 0, 0)) for block in blocks),
        name="weights_ahead",
    )(*data)

    home_bits, steps = split_bits(count)
    spread_shape = shape(sections << len(home_bits), 4, width, dtype=F32)
    totals = []
    part = (own, swap_far(far_out), swap_near(near_out))
    for layer in reversed(range(top)):
        weight_specs = [pl.BlockSpec(b, lambda *_, at=layer: (at, 0, 0, 0, 0)) for b in blocks]
        total, mods, own, far_out, near_out, *spread = run(
            functools.partial(lower_layer, layer),
            data + part + tuple(weights) + (mods,),
            [shape(ROWS, width), chain[3]] + chain[:3] + ([] if layer else [spread_shape]),
            layer_specs(lambda *_, at=layer: at) + like(part) + weight_specs + like([mods]),
            flops=flops,
            name="lower_layer",
        )
        part = (own, swap_far(far_out), swap_near(near_out))
        totals.append(total)

    mods_shape = shape(1, 4, sections * width, dtype=F32)
    out, mods = run(
        gather_totals,
        part + tuple(reversed(totals)) + (home_and_sum(spread[0]),),
        [shape(sections, ROWS, width), mods_shape],
        name="gather_totals",
    )
    received = lax.all_to_all(out, "section", 0, 0, tiled=True)
    for bits in steps[:-1]:
        (mods,) = run(add_group, (mods, *group_moves(mods, bits)), [mods_shape], name="add_group")
    return tuple(
        run(
            finish,
            (received, mods, *group_moves(mods, steps[-1])),
            [shape(*video_saved.shape), shape(*audio_saved.shape), mods_shape],
            name="finish",
        )
    )


def solution(mesh):
    return jax.shard_map(
        local,
        mesh=mesh,
        in_specs=(
            P("section", None, "seq", None),
            P("section", None, "seq", None),
            P(None, "seq", None),
            P(None, "seq", None),
            P("section", None, None),
            P("seq", None),
            P("seq", None),
        ),
        out_specs=(
            P("section", None, "seq", None),
            P("section", None, "seq", None),
            P("section", None, None),
        ),
        check_vma=False,
    )
```

time: 705 us -> 109 us (0.15); the launches traced: 692 us -> 109 us
  blocking collectives: 281 us -> 0 us
  starting transfers between devices: 162 us -> 43.5 us
  local copies, waits for them, and re-layouts: 72 us -> 1.94 us
  matrix products: 67.8 us -> 0 us
  other arithmetic: 31.8 us -> 0 us
  waiting for transfers between devices: 72.7 us -> 52.1 us
  Pallas kernels: 0 us -> 10.5 us
    psum x1 -> x0, blocking collectives: 281 us -> none  [local(): mod_summed = lax.psum(mod_total, 'seq')]
    ppermute x48 -> x19, starting transfers between devices: 162 us -> 34.1 us  [the longest x10 15.4 us: swap(): return lax.ppermute(value, 'seq', pairs + [(b, a) for a, b in pairs])]
    dot_general x60 -> x0, matrix products: 67.8 us -> none  [the longest x30 36 us: cross_attend(): mixed = jnp.einsum('hqk,khd->qhd', weights, value_heads, precision=precise)]
    unnamed x452 -> x14, local copies, waits for them, and re-layouts: 35.2 us -> 1.94 us
    ppermute x48 -> x19, waiting for transfers between devices: 72.7 us -> 49.5 us  [the longest x10 35 us: swap(): return lax.ppermute(value, 'seq', pairs + [(b, a) for a, b in pairs])]
    reshape x36 -> x0, local copies, waits for them, and re-layouts: 17.2 us -> none  [the longest x4 3.89 us: block_layer(): mods[3] * audio_mixed]
    pallas_call x0 -> x11, Pallas kernels: none -> 10.5 us  [the longest x8 5.85 us: run(): call(body, tuple(outs), grid=(1,), in_specs=specs or like(arrays), out_sp...]
    reduce_sum x18 -> x0, other arithmetic: 9.47 us -> none  [the longest x4 5.3 us: block_layer(): mods[2] * video_mixed]
  transfers between devices with their start and end apart: 48 -> 21, of which waited for: 18 -> 14; matrix products, arithmetic and copies ran while one was open for 16% -> 0% of each run, Pallas kernels for 0% -> 2%
where the time goes in v1:
time: 109 us
  waiting for transfers between devices  52.1 us (48%)
  starting transfers between devices  43.5 us (40%)
  Pallas kernels  10.5 us (10%)
  local copies, waits for them, and re-layouts  1.94 us (2%)
    ppermute x10, waiting for transfers between devices, swap(): return lax.ppermute(value, 'seq', pairs + [(b, a) for a, b in pairs])  35 us
    ppermute x10, starting transfers between devices, swap(): return lax.ppermute(value, 'seq', pairs + [(b, a) for a, b in pairs])  15.4 us
    ppermute x3, starting transfers between devices, to_section(): lax.ppermute(value, 'section', [(s, (s + k) % count) for s in range(count)])  10.5 us
    ppermute x3, waiting for transfers between devices, to_section(): lax.ppermute(value, 'section', [(s, (s + k) % count) for s in range(count)])  10.4 us
    ppermute x6, starting transfers between devices, group_moves(): lax.ppermute(value, 'seq', [(i, i ^ mask) for i in range(count)])  8.26 us
    pallas_call x8, Pallas kernels, run(): call(body, tuple(outs), grid=(1,), in_specs=specs or like(arrays), out_sp...  5.85 us
    all_to_all x1, starting transfers between devices, local(): received = lax.all_to_all(out, 'section', 0, 0, tiled=True)  5.61 us
    ppermute x6, waiting for transfers between devices, group_moves(): lax.ppermute(value, 'seq', [(i, i ^ mask) for i in range(count)])  4.12 us
  transfers between devices with their start and end apart: 21, of which 14 were waited for; matrix products, arithmetic and copies ran while one was open for 0% of the time, Pallas kernels for 2%

profile of v1, /device:TPU:32, one launch (start us, length us, event | category | flops | bytes accessed | tf_op | source)
XLA Modules:
  0.0 108.8 jit_solution(501167368543354377)
XLA Ops:
  0.7 2.0 %prepare.1 = (bf16[208,384]{1,0:T(8,128)(2,1)}, bf16[208,384]{1,0:T(8,128)(2,1)}, bf16[208,384]{1,0:T(8,128)(2,1)}) custom-call(bf16[1,2,64,1536]{3,2,1,0:T(8,128)(2,1)} %refs_0_.3, bf16[1,2,32,1536]{3,2,1,0:T(8,128)(2,1)} %refs_1_.3, f32[1,4,1536]{2,1,0:T(4,128)} %refs_2_.3, s32[1,2]{1,0:T(1,128)} %refs_3_.3, s32[1,2]{1,0:T(1,128)} %refs_4_.3), custom_call_target="tpu_custom_call" | custom-call | bytes 1048576 | tf_op jit(solution)/shard_map/prepare/pallas_call | solution.py:414
  2.7 3.3 %collective-permute-start = (bf16[208,384]{1,0:T(8,128)(2,1)}, bf16[208,384]{1,0:T(8,128)(2,1)S(1)}, u32[]{:S(2)}, u32[]{:S(2)}) collective-permute-start(bf16[208,384]{1,0:T(8,128)(2,1)} %get-tuple-element.34), channel_id=1, source_target_pairs={{0,64},{64,128},{128,192},{192,0},{1,65},{65,129},{129,193},{193,1... | collective-permute-start | bytes 479240 | tf_op jit(solution)/shard_map/ppermute | solution.py:359
  6.0 2.2 %collective-permute-start.1 = (bf16[208,384]{1,0:T(8,128)(2,1)}, bf16[208,384]{1,0:T(8,128)(2,1)S(1)}, u32[]{:S(2)}, u32[]{:S(2)}) collective-permute-start(bf16[208,384]{1,0:T(8,128)(2,1)} %get-tuple-element.35), channel_id=1, source_target_pairs={{0,192},{64,0},{128,64},{192,128},{1,193},{65,1},{129,65},{193,129... | collective-permute-start | bytes 479240 | tf_op jit(solution)/shard_map/ppermute | solution.py:359
  8.3 4.9 %collective-permute-start.2 = (bf16[208,384]{1,0:T(8,128)(2,1)}, bf16[208,384]{1,0:T(8,128)(2,1)S(1)}, u32[]{:S(2)}, u32[]{:S(2)}) collective-permute-start(bf16[208,384]{1,0:T(8,128)(2,1)} %get-tuple-element.36), channel_id=1, source_target_pairs={{0,128},{64,192},{128,0},{192,64},{1,129},{65,193},{129,1},{193,65... | collective-permute-start | bytes 479240 | tf_op jit(solution)/shard_map/ppermute | solution.py:359
  13.2 1.0 copy-done.2
  14.2 0.9 copy-done.3
  15.1 1.1 %prepare_own.1 = (bf16[208,384]{1,0:T(8,128)(2,1)S(1)}, bf16[192,384]{1,0:T(8,128)(2,1)S(1)}) custom-call(bf16[1,2,64,1536]{3,2,1,0:T(8,128)(2,1)S(1)} %copy-done, bf16[1,2,32,1536]{3,2,1,0:T(8,128)(2,1)S(1)} %copy-done.1, f32[1,4,1536]{2,1,0:T(4,128)S(1)} %copy-done.4, s32[1,2]{1,0:T(1,128)S(1)} %copy-done.5, s32[1,2]{1,0:T(1,128)S(1)} %copy-done.6, ...), custom_call_target="tpu_custom_call" | custom-call | bytes 1048576 | tf_op jit(solution)/shard_map/prepare_own/pallas_call | solution.py:414
  16.3 0.9 collective-permute-done.refs_0_
  17.2 9.5 %collective-permute-done.2.refs_2_ = bf16[208,384]{1,0:T(8,128)(2,1)S(1)} collective-permute-done((bf16[208,384]{1,0:T(8,128)(2,1)}, bf16[208,384]{1,0:T(8,128)(2,1)S(1)}, u32[]{:S(2)}, u32[]{:S(2)}) %collective-permute-start.2) | collective-permute-done | bytes 159776 | tf_op jit(solution)/shard_map/ppermute | solution.py:359
  26.7 1.9 %collective-permute-start.3 = (bf16[4,96,384]{2,1,0:T(8,128)(2,1)S(1)}, bf16[4,96,384]{2,1,0:T(8,128)(2,1)S(1)}, u32[]{:S(2)}, u32[]{:S(2)}) collective-permute-start(bf16[4,96,384]{2,1,0:T(8,128)(2,1)S(1)} %get-tuple-element.38.far_own.refs_0_), channel_id=1, source_target_pairs={{1,2},{3,4},{5,6},{7,8},{9,10},{11,12},{13,14},{15,16},{17,18},{19... | collective-permute-start | bytes 884744 | tf_op jit(solution)/shard_map/ppermute | solution.py:344
  28.6 1.8 %collective-permute-start.4 = (bf16[4,96,384]{2,1,0:T(8,128)(2,1)S(1)}, bf16[4,96,384]{2,1,0:T(8,128)(2,1)S(1)}, u32[]{:S(2)}, u32[]{:S(2)}) collective-permute-start(bf16[4,96,384]{2,1,0:T(8,128)(2,1)S(1)} %get-tuple-element.39.near_own.refs_1_), channel_id=1, source_target_pairs={{0,1},{2,3},{4,5},{6,7},{8,9},{10,11},{12,13},{14,15},{16,17},{18,... | collective-permute-start | bytes 884744 | tf_op jit(solution)/shard_map/ppermute | solution.py:344
  30.4 8.6 %collective-permute-done.3.far_in.refs_2_ = bf16[4,96,384]{2,1,0:T(8,128)(2,1)S(1)} collective-permute-done((bf16[4,96,384]{2,1,0:T(8,128)(2,1)S(1)}, bf16[4,96,384]{2,1,0:T(8,128)(2,1)S(1)}, u32[]{:S(2)}, u32[]{:S(2)}) %collective-permute-start.3) | collective-permute-done | bytes 294944 | tf_op jit(solution)/shard_map/ppermute | solution.py:344
  39.0 1.0 top_layer.1
  40.0 1.9 %collective-permute-start.5 = (bf16[96,384]{1,0:T(8,128)(2,1)S(1)}, bf16[96,384]{1,0:T(8,128)(2,1)S(1)}, u32[]{:S(2)}, u32[]{:S(2)}) collective-permute-start(bf16[96,384]{1,0:T(8,128)(2,1)S(1)} %get-tuple-element.43), channel_id=1, source_target_pairs={{1,2},{3,4},{5,6},{7,8},{9,10},{11,12},{13,14},{15,16},{17,18},{19... | collective-permute-start | bytes 221192 | tf_op jit(solution)/shard_map/ppermute | solution.py:344
  42.0 1.5 %weights_ahead.1 = (f32[3,2,3,64,64]{4,3,2,1,0:T(8,128)S(1)}, f32[3,2,3,32,128]{4,3,2,1,0:T(8,128)S(1)}) custom-call(bf16[4,96,384]{2,1,0:T(8,128)(2,1)S(1)} %get-tuple-element.38.far_own.refs_0_, bf16[4,96,384]{2,1,0:T(8,128)(2,1)S(1)} %get-tuple-element.39.near_own.refs_1_, bf16[4,96,384]{2,1,0:T(8,128)(2,1)S(1)} %collective-permute-done.3.far_in.refs_2_, ...), custom_call_target="tpu_custom_call" | custom-call | flops 600000000 | bytes 1048576 | tf_op jit(solution)/shard_map/weights_ahead/pallas_call | solution.py:466
  43.5 6.4 %collective-permute-done.5.refs_6_ = bf16[96,384]{1,0:T(8,128)(2,1)S(1)} collective-permute-done((bf16[96,384]{1,0:T(8,128)(2,1)S(1)}, bf16[96,384]{1,0:T(8,128)(2,1)S(1)}, u32[]{:S(2)}, u32[]{:S(2)}) %collective-permute-start.5) | collective-permute-done | bytes 73760 | tf_op jit(solution)/shard_map/ppermute | solution.py:344
  50.7 1.9 %collective-permute-start.7 = (bf16[96,384]{1,0:T(8,128)(2,1)S(1)}, bf16[96,384]{1,0:T(8,128)(2,1)S(1)}, u32[]{:S(2)}, u32[]{:S(2)}) collective-permute-start(bf16[96,384]{1,0:T(8,128)(2,1)S(1)} %get-tuple-element.49), channel_id=1, source_target_pairs={{1,2},{3,4},{5,6},{7,8},{9,10},{11,12},{13,14},{15,16},{17,18},{19... | collective-permute-start | bytes 221192 | tf_op jit(solution)/shard_map/ppermute | solution.py:344
  52.7 7.9 %collective-permute-done.7.refs_6_ = bf16[96,384]{1,0:T(8,128)(2,1)S(1)} collective-permute-done((bf16[96,384]{1,0:T(8,128)(2,1)S(1)}, bf16[96,384]{1,0:T(8,128)(2,1)S(1)}, u32[]{:S(2)}, u32[]{:S(2)}) %collective-permute-start.7) | collective-permute-done | bytes 73760 | tf_op jit(solution)/shard_map/ppermute | solution.py:344
  61.4 1.9 %collective-permute-start.9 = (bf16[96,384]{1,0:T(8,128)(2,1)S(1)}, bf16[96,384]{1,0:T(8,128)(2,1)S(1)}, u32[]{:S(2)}, u32[]{:S(2)}) collective-permute-start(bf16[96,384]{1,0:T(8,128)(2,1)S(1)} %get-tuple-element.53), channel_id=1, source_target_pairs={{1,2},{3,4},{5,6},{7,8},{9,10},{11,12},{13,14},{15,16},{17,18},{19... | collective-permute-start | bytes 221192 | tf_op jit(solution)/shard_map/ppermute | solution.py:344
  63.4 7.9 %collective-permute-done.9.refs_6_ = bf16[96,384]{1,0:T(8,128)(2,1)S(1)} collective-permute-done((bf16[96,384]{1,0:T(8,128)(2,1)S(1)}, bf16[96,384]{1,0:T(8,128)(2,1)S(1)}, u32[]{:S(2)}, u32[]{:S(2)}) %collective-permute-start.9) | collective-permute-done | bytes 73760 | tf_op jit(solution)/shard_map/ppermute | solution.py:344
  71.3 1.4 %lower_layer.5 = (bf16[192,384]{1,0:T(8,128)(2,1)S(1)}, f32[4,4,384]{2,1,0:T(4,128)}, f32[192,384]{1,0:T(8,128)S(1)}, bf16[96,384]{1,0:T(8,128)(2,1)S(1)}, bf16[...) custom-call(bf16[4,96,384]{2,1,0:T(8,128)(2,1)S(1)} %get-tuple-element.38.far_own.refs_0_, ...), custom_call_target="tpu_custom_call" | custom-call | flops 200000000 | bytes 1048576 | tf_op jit(solution)/shard_map/lower_layer/pallas_call | solution.py:402
  72.7 3.7 %all-to-all-start = ((f32[16,4,384]{2,1,0:T(4,128)}), f32[16,4,384]{2,1,0:T(4,128)S(1)}, u32[]{:S(2)}, u32[]{:S(2)}) async-start(f32[16,4,384]{2,1,0:T(4,128)} %get-tuple-element.62), calls=%async_computation | async-start | bytes 196608 | tf_op jit(solution)/shard_map/all_to_all | solution.py:376
  76.4 5.6 %collective-permute-start.11 = (bf16[96,384]{1,0:T(8,128)(2,1)S(1)}, bf16[96,384]{1,0:T(8,128)(2,1)S(1)}, u32[]{:S(2)}, u32[]{:S(2)}) collective-permute-start(bf16[96,384]{1,0:T(8,128)(2,1)S(1)} %get-tuple-element.57), channel_id=1, source_target_pairs={{1,2},{3,4},{5,6},{7,8},{9,10},{11,12},{13,14},{15,16},{17,18},{19... | collective-permute-start | bytes 221192 | tf_op jit(solution)/shard_map/ppermute | solution.py:344
  82.1 4.3 %collective-permute-done.11.far_part = bf16[96,384]{1,0:T(8,128)(2,1)S(1)} collective-permute-done((bf16[96,384]{1,0:T(8,128)(2,1)S(1)}, bf16[96,384]{1,0:T(8,128)(2,1)S(1)}, u32[]{:S(2)}, u32[]{:S(2)}) %collective-permute-start.11) | collective-permute-done | bytes 73760 | tf_op jit(solution)/shard_map/ppermute | solution.py:344
  86.4 0.9 gather_totals.1
  87.3 5.6 %all-to-all-start.1 = ((bf16[4,192,384]{2,1,0:T(8,128)(2,1)}), bf16[4,192,384]{2,1,0:T(8,128)(2,1)S(1)}, u32[]{:S(2)}, u32[]{:S(2)}) async-start(bf16[4,192,384]{2,1,0:T(8,128)(2,1)} %get-tuple-element.63), calls=%async_computation.1 | async-start | bytes 1179648 | tf_op jit(solution)/shard_map/all_to_all | solution.py:500
  92.9 4.1 %collective-permute-start.13 = (f32[1,4,1536]{2,1,0:T(4,128)S(1)}, f32[1,4,1536]{2,1,0:T(4,128)S(1)}, u32[]{:S(2)}, u32[]{:S(2)}) collective-permute-start(f32[1,4,1536]{2,1,0:T(4,128)S(1)} %get-tuple-element.64.own), channel_id=1, source_target_pairs={{0,2},{1,3},{2,0},{3,1},{4,6},{5,7},{6,4},{7,5},{8,10},{9,11},{10,... | collective-permute-start | bytes 73736 | tf_op jit(solution)/shard_map/ppermute | solution.py:386
  97.0 0.9 collective-permute-done.15.refs_2_
  99.3 4.0 %collective-permute-start.16 = (f32[1,4,1536]{2,1,0:T(4,128)S(1)}, f32[1,4,1536]{2,1,0:T(4,128)S(1)}, u32[]{:S(2)}, u32[]{:S(2)}) collective-permute-start(f32[1,4,1536]{2,1,0:T(4,128)S(1)} %add_group.1.mods), channel_id=1, source_target_pairs={{0,8},{1,9},{2,10},{3,11},{4,12},{5,13},{6,14},{7,15},{8,0},{9,1},... | collective-permute-start | bytes 73736 | tf_op jit(solution)/shard_map/ppermute | solution.py:386
  103.3 0.9 collective-permute-done.18.refs_2_
  105.3 2.6 %all-to-all-done.1.received = bf16[4,192,384]{2,1,0:T(8,128)(2,1)S(1)} async-done(((bf16[4,192,384]{2,1,0:T(8,128)(2,1)}), bf16[4,192,384]{2,1,0:T(8,128)(2,1)S(1)}, u32[]{:S(2)}, u32[]{:S(2)}) %all-to-all-start.1) | async-done | bytes 589856 | tf_op jit(solution)/shard_map/all_to_all | solution.py:500
  107.9 0.9 finish.1
  (35 shorter events, 4.6 us)
Async XLA Ops:
  0.6 12.5 %copy-start.4 = (f32[1,4,1536]{2,1,0:T(4,128)S(1)}, f32[1,4,1536]{2,1,0:T(4,128)}, u32[]{:S(2)}) copy-start(f32[1,4,1536]{2,1,0:T(4,128)} %refs_2_.3) | copy-start | bytes 73732
  0.6 12.5 %copy-start.1 = (bf16[1,2,32,1536]{3,2,1,0:T(8,128)(2,1)S(1)}, bf16[1,2,32,1536]{3,2,1,0:T(8,128)(2,1)}, u32[]{:S(2)}) copy-start(bf16[1,2,32,1536]{3,2,1,0:T(8,128)(2,1)} %refs_1_.3) | copy-start | bytes 589828
  0.7 12.5 %copy-start = (bf16[1,2,64,1536]{3,2,1,0:T(8,128)(2,1)S(1)}, bf16[1,2,64,1536]{3,2,1,0:T(8,128)(2,1)}, u32[]{:S(2)}) copy-start(bf16[1,2,64,1536]{3,2,1,0:T(8,128)(2,1)} %refs_0_.3) | copy-start | bytes 1179652
  2.7 14.5 %collective-permute-start = (bf16[208,384]{1,0:T(8,128)(2,1)}, bf16[208,384]{1,0:T(8,128)(2,1)S(1)}, u32[]{:S(2)}, u32[]{:S(2)}) collective-permute-start(bf16[208,384]{1,0:T(8,128)(2,1)} %get-tuple-element.34), channel_id=1, source_target_pairs={{0,64},{64,128},{128,192},{192,0},{1,65},{65,129},{129,193},{193,1... | collective-permute-start | bytes 479240 | tf_op jit(solution)/shard_map/ppermute | solution.py:359
  6.0 7.2 %copy-start.5 = (s32[1,2]{1,0:T(1,128)S(1)}, s32[1,2]{1,0:T(1,128)}, u32[]{:S(2)}) copy-start(s32[1,2]{1,0:T(1,128)} %refs_3_.3) | copy-start | bytes 28
  6.0 7.2 %copy-start.6 = (s32[1,2]{1,0:T(1,128)S(1)}, s32[1,2]{1,0:T(1,128)}, u32[]{:S(2)}) copy-start(s32[1,2]{1,0:T(1,128)} %refs_4_.3) | copy-start | bytes 28
  6.0 11.2 %collective-permute-start.1 = (bf16[208,384]{1,0:T(8,128)(2,1)}, bf16[208,384]{1,0:T(8,128)(2,1)S(1)}, u32[]{:S(2)}, u32[]{:S(2)}) collective-permute-start(bf16[208,384]{1,0:T(8,128)(2,1)} %get-tuple-element.35), channel_id=1, source_target_pairs={{0,192},{64,0},{128,64},{192,128},{1,193},{65,1},{129,65},{193,129... | collective-permute-start | bytes 479240 | tf_op jit(solution)/shard_map/ppermute | solution.py:359
  8.3 18.4 %collective-permute-start.2 = (bf16[208,384]{1,0:T(8,128)(2,1)}, bf16[208,384]{1,0:T(8,128)(2,1)S(1)}, u32[]{:S(2)}, u32[]{:S(2)}) collective-permute-start(bf16[208,384]{1,0:T(8,128)(2,1)} %get-tuple-element.36), channel_id=1, source_target_pairs={{0,128},{64,192},{128,0},{192,64},{1,129},{65,193},{129,1},{193,65... | collective-permute-start | bytes 479240 | tf_op jit(solution)/shard_map/ppermute | solution.py:359
  13.2 1.0 copy-start.2
  14.2 0.9 copy-start.3
  26.7 12.3 %collective-permute-start.3 = (bf16[4,96,384]{2,1,0:T(8,128)(2,1)S(1)}, bf16[4,96,384]{2,1,0:T(8,128)(2,1)S(1)}, u32[]{:S(2)}, u32[]{:S(2)}) collective-permute-start(bf16[4,96,384]{2,1,0:T(8,128)(2,1)S(1)} %get-tuple-element.38.far_own.refs_0_), channel_id=1, source_target_pairs={{1,2},{3,4},{5,6},{7,8},{9,10},{11,12},{13,14},{15,16},{17,18},{19... | collective-permute-start | bytes 884744 | tf_op jit(solution)/shard_map/ppermute | solution.py:344
  28.6 10.3 %collective-permute-start.4 = (bf16[4,96,384]{2,1,0:T(8,128)(2,1)S(1)}, bf16[4,96,384]{2,1,0:T(8,128)(2,1)S(1)}, u32[]{:S(2)}, u32[]{:S(2)}) collective-permute-start(bf16[4,96,384]{2,1,0:T(8,128)(2,1)S(1)} %get-tuple-element.39.near_own.refs_1_), channel_id=1, source_target_pairs={{0,1},{2,3},{4,5},{6,7},{8,9},{10,11},{12,13},{14,15},{16,17},{18,... | collective-permute-start | bytes 884744 | tf_op jit(solution)/shard_map/ppermute | solution.py:344
  40.0 9.9 %collective-permute-start.5 = (bf16[96,384]{1,0:T(8,128)(2,1)S(1)}, bf16[96,384]{1,0:T(8,128)(2,1)S(1)}, u32[]{:S(2)}, u32[]{:S(2)}) collective-permute-start(bf16[96,384]{1,0:T(8,128)(2,1)S(1)} %get-tuple-element.43), channel_id=1, source_target_pairs={{1,2},{3,4},{5,6},{7,8},{9,10},{11,12},{13,14},{15,16},{17,18},{19... | collective-permute-start | bytes 221192 | tf_op jit(solution)/shard_map/ppermute | solution.py:344
  41.9 8.0 %collective-permute-start.6 = (bf16[96,384]{1,0:T(8,128)(2,1)S(1)}, bf16[96,384]{1,0:T(8,128)(2,1)S(1)}, u32[]{:S(2)}, u32[]{:S(2)}) collective-permute-start(bf16[96,384]{1,0:T(8,128)(2,1)S(1)} %get-tuple-element.44), channel_id=1, source_target_pairs={{0,1},{2,3},{4,5},{6,7},{8,9},{10,11},{12,13},{14,15},{16,17},{18,... | collective-permute-start | bytes 221192 | tf_op jit(solution)/shard_map/ppermute | solution.py:344
  50.7 9.9 %collective-permute-start.7 = (bf16[96,384]{1,0:T(8,128)(2,1)S(1)}, bf16[96,384]{1,0:T(8,128)(2,1)S(1)}, u32[]{:S(2)}, u32[]{:S(2)}) collective-permute-start(bf16[96,384]{1,0:T(8,128)(2,1)S(1)} %get-tuple-element.49), channel_id=1, source_target_pairs={{1,2},{3,4},{5,6},{7,8},{9,10},{11,12},{13,14},{15,16},{17,18},{19... | collective-permute-start | bytes 221192 | tf_op jit(solution)/shard_map/ppermute | solution.py:344
  52.6 8.0 %collective-permute-start.8 = (bf16[96,384]{1,0:T(8,128)(2,1)S(1)}, bf16[96,384]{1,0:T(8,128)(2,1)S(1)}, u32[]{:S(2)}, u32[]{:S(2)}) collective-permute-start(bf16[96,384]{1,0:T(8,128)(2,1)S(1)} %get-tuple-element.50), channel_id=1, source_target_pairs={{0,1},{2,3},{4,5},{6,7},{8,9},{10,11},{12,13},{14,15},{16,17},{18,... | collective-permute-start | bytes 221192 | tf_op jit(solution)/shard_map/ppermute | solution.py:344
  61.4 9.9 %collective-permute-start.9 = (bf16[96,384]{1,0:T(8,128)(2,1)S(1)}, bf16[96,384]{1,0:T(8,128)(2,1)S(1)}, u32[]{:S(2)}, u32[]{:S(2)}) collective-permute-start(bf16[96,384]{1,0:T(8,128)(2,1)S(1)} %get-tuple-element.53), channel_id=1, source_target_pairs={{1,2},{3,4},{5,6},{7,8},{9,10},{11,12},{13,14},{15,16},{17,18},{19... | collective-permute-start | bytes 221192 | tf_op jit(solution)/shard_map/ppermute | solution.py:344
  63.3 8.0 %collective-permute-start.10 = (bf16[96,384]{1,0:T(8,128)(2,1)S(1)}, bf16[96,384]{1,0:T(8,128)(2,1)S(1)}, u32[]{:S(2)}, u32[]{:S(2)}) collective-permute-start(bf16[96,384]{1,0:T(8,128)(2,1)S(1)} %get-tuple-element.54), channel_id=1, source_target_pairs={{0,1},{2,3},{4,5},{6,7},{8,9},{10,11},{12,13},{14,15},{16,17},{18,... | collective-permute-start | bytes 221192 | tf_op jit(solution)/shard_map/ppermute | solution.py:344
  72.7 13.7 %all-to-all-start = ((f32[16,4,384]{2,1,0:T(4,128)}), f32[16,4,384]{2,1,0:T(4,128)S(1)}, u32[]{:S(2)}, u32[]{:S(2)}) async-start(f32[16,4,384]{2,1,0:T(4,128)} %get-tuple-element.62), calls=%async_computation | async-start | bytes 196608 | tf_op jit(solution)/shard_map/all_to_all | solution.py:376
  76.4 10.0 %collective-permute-start.11 = (bf16[96,384]{1,0:T(8,128)(2,1)S(1)}, bf16[96,384]{1,0:T(8,128)(2,1)S(1)}, u32[]{:S(2)}, u32[]{:S(2)}) collective-permute-start(bf16[96,384]{1,0:T(8,128)(2,1)S(1)} %get-tuple-element.57), channel_id=1, source_target_pairs={{1,2},{3,4},{5,6},{7,8},{9,10},{11,12},{13,14},{15,16},{17,18},{19... | collective-permute-start | bytes 221192 | tf_op jit(solution)/shard_map/ppermute | solution.py:344
  82.0 4.4 %collective-permute-start.12 = (bf16[96,384]{1,0:T(8,128)(2,1)S(1)}, bf16[96,384]{1,0:T(8,128)(2,1)S(1)}, u32[]{:S(2)}, u32[]{:S(2)}) collective-permute-start(bf16[96,384]{1,0:T(8,128)(2,1)S(1)} %get-tuple-element.58), channel_id=1, source_target_pairs={{0,1},{2,3},{4,5},{6,7},{8,9},{10,11},{12,13},{14,15},{16,17},{18,... | collective-permute-start | bytes 221192 | tf_op jit(solution)/shard_map/ppermute | solution.py:344
  87.3 20.6 %all-to-all-start.1 = ((bf16[4,192,384]{2,1,0:T(8,128)(2,1)}), bf16[4,192,384]{2,1,0:T(8,128)(2,1)S(1)}, u32[]{:S(2)}, u32[]{:S(2)}) async-start(bf16[4,192,384]{2,1,0:T(8,128)(2,1)} %get-tuple-element.63), calls=%async_computation.1 | async-start | bytes 1179648 | tf_op jit(solution)/shard_map/all_to_all | solution.py:500
  92.9 5.0 %collective-permute-start.15 = (f32[1,4,1536]{2,1,0:T(4,128)S(1)}, f32[1,4,1536]{2,1,0:T(4,128)S(1)}, u32[]{:S(2)}, u32[]{:S(2)}) collective-permute-start(f32[1,4,1536]{2,1,0:T(4,128)S(1)} %get-tuple-element.64.own), channel_id=1, source_target_pairs={{0,6},{1,7},{2,4},{3,5},{4,2},{5,3},{6,0},{7,1},{8,14},{9,15},{10,... | collective-permute-start | bytes 73736 | tf_op jit(solution)/shard_map/ppermute | solution.py:386
  92.9 5.3 %collective-permute-start.14 = (f32[1,4,1536]{2,1,0:T(4,128)S(1)}, f32[1,4,1536]{2,1,0:T(4,128)S(1)}, u32[]{:S(2)}, u32[]{:S(2)}) collective-permute-start(f32[1,4,1536]{2,1,0:T(4,128)S(1)} %get-tuple-element.64.own), channel_id=1, source_target_pairs={{0,4},{1,5},{2,6},{3,7},{4,0},{5,1},{6,2},{7,3},{8,12},{9,13},{10,... | collective-permute-start | bytes 73736 | tf_op jit(solution)/shard_map/ppermute | solution.py:386
  92.9 6.1 %collective-permute-start.13 = (f32[1,4,1536]{2,1,0:T(4,128)S(1)}, f32[1,4,1536]{2,1,0:T(4,128)S(1)}, u32[]{:S(2)}, u32[]{:S(2)}) collective-permute-start(f32[1,4,1536]{2,1,0:T(4,128)S(1)} %get-tuple-element.64.own), channel_id=1, source_target_pairs={{0,2},{1,3},{2,0},{3,1},{4,6},{5,7},{6,4},{7,5},{8,10},{9,11},{10,... | collective-permute-start | bytes 73736 | tf_op jit(solution)/shard_map/ppermute | solution.py:386
  99.1 5.1 %collective-permute-start.18 = (f32[1,4,1536]{2,1,0:T(4,128)S(1)}, f32[1,4,1536]{2,1,0:T(4,128)S(1)}, u32[]{:S(2)}, u32[]{:S(2)}) collective-permute-start(f32[1,4,1536]{2,1,0:T(4,128)S(1)} %add_group.1.mods), channel_id=1, source_target_pairs={{0,24},{1,25},{2,26},{3,27},{4,28},{5,29},{6,30},{7,31},{8,16},{9,... | collective-permute-start | bytes 73736 | tf_op jit(solution)/shard_map/ppermute | solution.py:386
  99.2 5.4 %collective-permute-start.17 = (f32[1,4,1536]{2,1,0:T(4,128)S(1)}, f32[1,4,1536]{2,1,0:T(4,128)S(1)}, u32[]{:S(2)}, u32[]{:S(2)}) collective-permute-start(f32[1,4,1536]{2,1,0:T(4,128)S(1)} %add_group.1.mods), channel_id=1, source_target_pairs={{0,16},{1,17},{2,18},{3,19},{4,20},{5,21},{6,22},{7,23},{8,24},{9,... | collective-permute-start | bytes 73736 | tf_op jit(solution)/shard_map/ppermute | solution.py:386
  99.3 6.0 %collective-permute-start.16 = (f32[1,4,1536]{2,1,0:T(4,128)S(1)}, f32[1,4,1536]{2,1,0:T(4,128)S(1)}, u32[]{:S(2)}, u32[]{:S(2)}) collective-permute-start(f32[1,4,1536]{2,1,0:T(4,128)S(1)} %add_group.1.mods), channel_id=1, source_target_pairs={{0,8},{1,9},{2,10},{3,11},{4,12},{5,13},{6,14},{7,15},{8,0},{9,1},... | collective-permute-start | bytes 73736 | tf_op jit(solution)/shard_map/ppermute | solution.py:386

commit v2 on v1

--- a/solution.py
+++ b/solution.py
@@ -285,7 +285,7 @@
         refs[4],
         refs[5:11],
     )
-    total_out, mods, *outs = refs[11:16]
+    total_out, mods, *outs = refs[11:]
     total = joined(own, far_part, near_part)
     total_out[...] = total
     mods[...] = mods_in[...]
@@ -296,10 +296,32 @@
         lambda kind, m, h: (v_weights, a_weights)[kind][0, m, h],
         outs,
     )
-    for spread in refs[16:]:
-        copies = spread.shape[0] // mods.shape[0]
-        for at in range(spread.shape[0]):
-            spread[at] = mods[at // copies]
+
+
+def ahead(mods, *refs):
+    totals, (home, spread) = refs[:-2], refs[-2:]
+    count = home.shape[0]
+    for at, total in enumerate(totals):
+        home[count - 1 - at] = total[...]
+    copies = spread.shape[0] // count
+    for at in range(spread.shape[0]):
+        spread[at] = mods[at // copies]
+
+
+def last_layer(*refs):
+    data, extra, (own, far_part, near_part, v_weights, a_weights) = refs[:4], refs[4], refs[5:10]
+    home, spread, *outs = refs[12:]
+    total = joined(own, far_part, near_part)
+    home[0] = total
+    found = backward_layer(
+        data,
+        extra,
+        total.astype(F32),
+        lambda kind, m, h: (v_weights, a_weights)[kind][0, m, h],
+        outs,
+    )
+    for at in range(spread.shape[0]):
+        spread[at] = found
 
 
 def group_sum(own, moved):
@@ -307,12 +329,9 @@
     return total + (moved[1][...] + moved[2][...]) if len(moved) == 3 else total
 
 
-def gather_totals(own, far_part, near_part, *refs):
-    totals, spread, out, mods = refs[:-3], *refs[-3:]
+def gather_totals(own, far_part, near_part, _, spread, out, mods):
     out[0] = joined(own, far_part, near_part)
-    for at, total in enumerate(totals):
-        out[at + 1] = total[...]
-    count = out.shape[0]
+    count = mods.shape[2] // own.shape[1]
     copies = spread.shape[0] // count
     chunks = []
     for c in range(count):
@@ -475,28 +494,53 @@
 
     home_bits, steps = split_bits(count)
     spread_shape = shape(sections << len(home_bits), 4, width, dtype=F32)
+    anywhere = pl.BlockSpec(memory_space=pl.ANY)
+    home_shape = shape(sections, ROWS, width)
+
+    def slot(at):
+        return pl.BlockSpec((1, ROWS, width), lambda *_: (at, 0, 0))
+
     totals = []
     part = (own, swap_far(far_out), swap_near(near_out))
     for layer in reversed(range(top)):
         weight_specs = [pl.BlockSpec(b, lambda *_, at=layer: (at, 0, 0, 0, 0)) for b in blocks]
-        total, mods, own, far_out, near_out, *spread = run(
-            functools.partial(lower_layer, layer),
-            data + part + tuple(weights) + (mods,),
-            [shape(ROWS, width), chain[3]] + chain[:3] + ([] if layer else [spread_shape]),
-            layer_specs(lambda *_, at=layer: at) + like(part) + weight_specs + like([mods]),
-            flops=flops,
-            name="lower_layer",
-        )
+        specs = layer_specs(lambda *_, at=layer: at) + like(part) + weight_specs
+        if layer:
+            total, mods, own, far_out, near_out = run(
+                functools.partial(lower_layer, layer),
+                data + part + tuple(weights) + (mods,),
+                [shape(ROWS, width), chain[3]] + chain[:3],
+                specs + like([mods]),
+                flops=flops,
+                name="lower_layer",
+            )
+            totals.append(total)
+        else:
+            home, spread = run(
+                ahead, (mods, *totals), [home_shape, spread_shape], name="ahead"
+            )
+            home, spread, own, far_out, near_out = call(
+                last_layer,
+                (home_shape, spread_shape, *chain[:3]),
+                flops=flops,
+                grid=(1,),
+                in_specs=specs + [anywhere] * 2,
+                out_specs=(slot(1), whole(1 << len(home_bits), 4, width), *like(chain[:3])),
+                input_output_aliases={10: 0, 11: 1},
+                name="last_layer",
+            )(*data, *part, *weights, home, spread)
         part = (own, swap_far(far_out), swap_near(near_out))
-        totals.append(total)
 
     mods_shape = shape(1, 4, sections * width, dtype=F32)
-    out, mods = run(
+    out, mods = call(
         gather_totals,
-        part + tuple(reversed(totals)) + (home_and_sum(spread[0]),),
-        [shape(sections, ROWS, width), mods_shape],
+        (home_shape, mods_shape),
+        grid=(1,),
+        in_specs=like(part) + [anywhere] + like([spread_shape]),
+        out_specs=(slot(0), *like([mods_shape])),
+        input_output_aliases={3: 0},
         name="gather_totals",
-    )
+    )(*part, home, home_and_sum(spread))
     received = lax.all_to_all(out, "section", 0, 0, tiled=True)
     for bits in steps[:-1]:
         (mods,) = run(add_group, (mods, *group_moves(mods, bits)), [mods_shape], name="add_group")

time: 109 us -> 109 us (level)
    pallas_call x0 -> x2, Pallas kernels: none -> 2 us  [the longest x1 1.3 us: local(): call(last_layer, (home_shape, spread_shape, *chain[:3]), flops=flops, gri...]
    pallas_call x8 -> x7, Pallas kernels: 5.85 us -> 4.44 us  [run(): call(body, tuple(outs), grid=(1,), in_specs=specs or like(arrays), out_sp...]
  transfers between devices with their start and end apart: 21 -> 21, of which waited for: 14 -> 14; matrix products, arithmetic and copies ran while one was open for 0% -> 0% of each run, Pallas kernels for 2% -> 3%
where the time goes in v2:
time: 109 us
  waiting for transfers between devices  51.3 us (47%)
  starting transfers between devices  43.5 us (40%)
  Pallas kernels  11 us (10%)
  local copies, waits for them, and re-layouts  1.94 us (2%)
    ppermute x10, waiting for transfers between devices, swap(): return lax.ppermute(value, 'seq', pairs + [(b, a) for a, b in pairs])  34.2 us
    ppermute x10, starting transfers between devices, swap(): return lax.ppermute(value, 'seq', pairs + [(b, a) for a, b in pairs])  15.4 us
    ppermute x3, starting transfers between devices, to_section(): lax.ppermute(value, 'section', [(s, (s + k) % count) for s in range(count)])  10.5 us
    ppermute x3, waiting for transfers between devices, to_section(): lax.ppermute(value, 'section', [(s, (s + k) % count) for s in range(count)])  10.4 us
    ppermute x6, starting transfers between devices, group_moves(): lax.ppermute(value, 'seq', [(i, i ^ mask) for i in range(count)])  8.26 us
    all_to_all x1, starting transfers between devices, local(): received = lax.all_to_all(out, 'section', 0, 0, tiled=True)  5.61 us
    pallas_call x7, Pallas kernels, run(): call(body, tuple(outs), grid=(1,), in_specs=specs or like(arrays), out_sp...  4.44 us
    ppermute x6, waiting for transfers between devices, group_moves(): lax.ppermute(value, 'seq', [(i, i ^ mask) for i in range(count)])  4.12 us
  transfers between devices with their start and end apart: 21, of which 14 were waited for; matrix products, arithmetic and copies ran while one was open for 0% of the time, Pallas kernels for 3%

profile of v2, /device:TPU:32, one launch (start us, length us, event | category | flops | bytes accessed | tf_op | source)
XLA Modules:
  0.0 108.5 jit_solution(8374857273311883559)
XLA Ops:
  0.7 2.0 %prepare.1 = (bf16[208,384]{1,0:T(8,128)(2,1)}, bf16[208,384]{1,0:T(8,128)(2,1)}, bf16[208,384]{1,0:T(8,128)(2,1)}) custom-call(bf16[1,2,64,1536]{3,2,1,0:T(8,128)(2,1)} %refs_0_.3, bf16[1,2,32,1536]{3,2,1,0:T(8,128)(2,1)} %refs_1_.3, f32[1,4,1536]{2,1,0:T(4,128)} %refs_2_.3, s32[1,2]{1,0:T(1,128)} %refs_3_.3, s32[1,2]{1,0:T(1,128)} %refs_4_.3), custom_call_target="tpu_custom_call" | custom-call | bytes 1048576 | tf_op jit(solution)/shard_map/prepare/pallas_call | solution.py:433
  2.7 3.3 %collective-permute-start = (bf16[208,384]{1,0:T(8,128)(2,1)}, bf16[208,384]{1,0:T(8,128)(2,1)S(1)}, u32[]{:S(2)}, u32[]{:S(2)}) collective-permute-start(bf16[208,384]{1,0:T(8,128)(2,1)} %get-tuple-element.36), channel_id=1, source_target_pairs={{0,64},{64,128},{128,192},{192,0},{1,65},{65,129},{129,193},{193,1... | collective-permute-start | bytes 479240 | tf_op jit(solution)/shard_map/ppermute | solution.py:378
  6.0 2.2 %collective-permute-start.1 = (bf16[208,384]{1,0:T(8,128)(2,1)}, bf16[208,384]{1,0:T(8,128)(2,1)S(1)}, u32[]{:S(2)}, u32[]{:S(2)}) collective-permute-start(bf16[208,384]{1,0:T(8,128)(2,1)} %get-tuple-element.37), channel_id=1, source_target_pairs={{0,192},{64,0},{128,64},{192,128},{1,193},{65,1},{129,65},{193,129... | collective-permute-start | bytes 479240 | tf_op jit(solution)/shard_map/ppermute | solution.py:378
  8.3 4.9 %collective-permute-start.2 = (bf16[208,384]{1,0:T(8,128)(2,1)}, bf16[208,384]{1,0:T(8,128)(2,1)S(1)}, u32[]{:S(2)}, u32[]{:S(2)}) collective-permute-start(bf16[208,384]{1,0:T(8,128)(2,1)} %get-tuple-element.38), channel_id=1, source_target_pairs={{0,128},{64,192},{128,0},{192,64},{1,129},{65,193},{129,1},{193,65... | collective-permute-start | bytes 479240 | tf_op jit(solution)/shard_map/ppermute | solution.py:378
  13.2 1.0 copy-done.2
  14.2 0.9 copy-done.3
  15.1 1.1 %prepare_own.1 = (bf16[208,384]{1,0:T(8,128)(2,1)S(1)}, bf16[192,384]{1,0:T(8,128)(2,1)S(1)}) custom-call(bf16[1,2,64,1536]{3,2,1,0:T(8,128)(2,1)S(1)} %copy-done, bf16[1,2,32,1536]{3,2,1,0:T(8,128)(2,1)S(1)} %copy-done.1, f32[1,4,1536]{2,1,0:T(4,128)S(1)} %copy-done.4, s32[1,2]{1,0:T(1,128)S(1)} %copy-done.5, s32[1,2]{1,0:T(1,128)S(1)} %copy-done.6, ...), custom_call_target="tpu_custom_call" | custom-call | bytes 1048576 | tf_op jit(solution)/shard_map/prepare_own/pallas_call | solution.py:433
  16.3 0.9 collective-permute-done.refs_0_
  17.2 9.5 %collective-permute-done.2.refs_2_ = bf16[208,384]{1,0:T(8,128)(2,1)S(1)} collective-permute-done((bf16[208,384]{1,0:T(8,128)(2,1)}, bf16[208,384]{1,0:T(8,128)(2,1)S(1)}, u32[]{:S(2)}, u32[]{:S(2)}) %collective-permute-start.2) | collective-permute-done | bytes 159776 | tf_op jit(solution)/shard_map/ppermute | solution.py:378
  26.7 1.9 %collective-permute-start.3 = (bf16[4,96,384]{2,1,0:T(8,128)(2,1)S(1)}, bf16[4,96,384]{2,1,0:T(8,128)(2,1)S(1)}, u32[]{:S(2)}, u32[]{:S(2)}) collective-permute-start(bf16[4,96,384]{2,1,0:T(8,128)(2,1)S(1)} %get-tuple-element.40.far_own.refs_0_), channel_id=1, source_target_pairs={{1,2},{3,4},{5,6},{7,8},{9,10},{11,12},{13,14},{15,16},{17,18},{19... | collective-permute-start | bytes 884744 | tf_op jit(solution)/shard_map/ppermute | solution.py:363
  28.6 1.8 %collective-permute-start.4 = (bf16[4,96,384]{2,1,0:T(8,128)(2,1)S(1)}, bf16[4,96,384]{2,1,0:T(8,128)(2,1)S(1)}, u32[]{:S(2)}, u32[]{:S(2)}) collective-permute-start(bf16[4,96,384]{2,1,0:T(8,128)(2,1)S(1)} %get-tuple-element.41.near_own.refs_1_), channel_id=1, source_target_pairs={{0,1},{2,3},{4,5},{6,7},{8,9},{10,11},{12,13},{14,15},{16,17},{18,... | collective-permute-start | bytes 884744 | tf_op jit(solution)/shard_map/ppermute | solution.py:363
  30.4 8.6 %collective-permute-done.3.far_in.refs_2_ = bf16[4,96,384]{2,1,0:T(8,128)(2,1)S(1)} collective-permute-done((bf16[4,96,384]{2,1,0:T(8,128)(2,1)S(1)}, bf16[4,96,384]{2,1,0:T(8,128)(2,1)S(1)}, u32[]{:S(2)}, u32[]{:S(2)}) %collective-permute-start.3) | collective-permute-done | bytes 294944 | tf_op jit(solution)/shard_map/ppermute | solution.py:363
  39.0 1.0 top_layer.1
  40.0 1.9 %collective-permute-start.5 = (bf16[96,384]{1,0:T(8,128)(2,1)S(1)}, bf16[96,384]{1,0:T(8,128)(2,1)S(1)}, u32[]{:S(2)}, u32[]{:S(2)}) collective-permute-start(bf16[96,384]{1,0:T(8,128)(2,1)S(1)} %get-tuple-element.45), channel_id=1, source_target_pairs={{1,2},{3,4},{5,6},{7,8},{9,10},{11,12},{13,14},{15,16},{17,18},{19... | collective-permute-start | bytes 221192 | tf_op jit(solution)/shard_map/ppermute | solution.py:363
  42.0 1.5 %weights_ahead.1 = (f32[3,2,3,64,64]{4,3,2,1,0:T(8,128)S(1)}, f32[3,2,3,32,128]{4,3,2,1,0:T(8,128)S(1)}) custom-call(bf16[4,96,384]{2,1,0:T(8,128)(2,1)S(1)} %get-tuple-element.40.far_own.refs_0_, bf16[4,96,384]{2,1,0:T(8,128)(2,1)S(1)} %get-tuple-element.41.near_own.refs_1_, bf16[4,96,384]{2,1,0:T(8,128)(2,1)S(1)} %collective-permute-done.3.far_in.refs_2_, ...), custom_call_target="tpu_custom_call" | custom-call | flops 600000000 | bytes 1048576 | tf_op jit(solution)/shard_map/weights_ahead/pallas_call | solution.py:485
  43.5 6.4 %collective-permute-done.5.refs_6_ = bf16[96,384]{1,0:T(8,128)(2,1)S(1)} collective-permute-done((bf16[96,384]{1,0:T(8,128)(2,1)S(1)}, bf16[96,384]{1,0:T(8,128)(2,1)S(1)}, u32[]{:S(2)}, u32[]{:S(2)}) %collective-permute-start.5) | collective-permute-done | bytes 73760 | tf_op jit(solution)/shard_map/ppermute | solution.py:363
  50.7 1.9 %collective-permute-start.7 = (bf16[96,384]{1,0:T(8,128)(2,1)S(1)}, bf16[96,384]{1,0:T(8,128)(2,1)S(1)}, u32[]{:S(2)}, u32[]{:S(2)}) collective-permute-start(bf16[96,384]{1,0:T(8,128)(2,1)S(1)} %get-tuple-element.51), channel_id=1, source_target_pairs={{1,2},{3,4},{5,6},{7,8},{9,10},{11,12},{13,14},{15,16},{17,18},{19... | collective-permute-start | bytes 221192 | tf_op jit(solution)/shard_map/ppermute | solution.py:363
  52.7 7.9 %collective-permute-done.7.refs_6_ = bf16[96,384]{1,0:T(8,128)(2,1)S(1)} collective-permute-done((bf16[96,384]{1,0:T(8,128)(2,1)S(1)}, bf16[96,384]{1,0:T(8,128)(2,1)S(1)}, u32[]{:S(2)}, u32[]{:S(2)}) %collective-permute-start.7) | collective-permute-done | bytes 73760 | tf_op jit(solution)/shard_map/ppermute | solution.py:363
  61.4 1.9 %collective-permute-start.9 = (bf16[96,384]{1,0:T(8,128)(2,1)S(1)}, bf16[96,384]{1,0:T(8,128)(2,1)S(1)}, u32[]{:S(2)}, u32[]{:S(2)}) collective-permute-start(bf16[96,384]{1,0:T(8,128)(2,1)S(1)} %get-tuple-element.55), channel_id=1, source_target_pairs={{1,2},{3,4},{5,6},{7,8},{9,10},{11,12},{13,14},{15,16},{17,18},{19... | collective-permute-start | bytes 221192 | tf_op jit(solution)/shard_map/ppermute | solution.py:363
  63.4 0.9 ahead.1
  64.3 7.0 %collective-permute-done.9.refs_6_ = bf16[96,384]{1,0:T(8,128)(2,1)S(1)} collective-permute-done((bf16[96,384]{1,0:T(8,128)(2,1)S(1)}, bf16[96,384]{1,0:T(8,128)(2,1)S(1)}, u32[]{:S(2)}, u32[]{:S(2)}) %collective-permute-start.9) | collective-permute-done | bytes 73760 | tf_op jit(solution)/shard_map/ppermute | solution.py:363
  71.3 1.3 %last_layer.1 = (bf16[4,192,384]{2,1,0:T(8,128)(2,1)}, f32[16,4,384]{2,1,0:T(4,128)}, f32[192,384]{1,0:T(8,128)S(1)}, bf16[96,384]{1,0:T(8,128)(2,1)S(1)}, bf16[96,384]{1,0:T(8,128)(2,1)S(1)}) custom-call(bf16[4,96,384]{2,1,0:T(8,128)(2,1)S(1)} %get-tuple-element.40.far_own.refs_0_, ...), custom_call_target="tpu_custom_call", output_to_operand_aliasing={{0}: (10, {}), {1}: (11, {})} | custom-call | flops 200000000 | bytes 1048576 | tf_op jit(solution)/shard_map/last_layer/pallas_call | solution.py:522
  72.6 3.7 %all-to-all-start = ((f32[16,4,384]{2,1,0:T(4,128)}), f32[16,4,384]{2,1,0:T(4,128)S(1)}, u32[]{:S(2)}, u32[]{:S(2)}) async-start(f32[16,4,384]{2,1,0:T(4,128)} %get-tuple-element.66), calls=%async_computation | async-start | bytes 196608 | tf_op jit(solution)/shard_map/all_to_all | solution.py:395
  76.3 5.5 %collective-permute-start.11 = (bf16[96,384]{1,0:T(8,128)(2,1)S(1)}, bf16[96,384]{1,0:T(8,128)(2,1)S(1)}, u32[]{:S(2)}, u32[]{:S(2)}) collective-permute-start(bf16[96,384]{1,0:T(8,128)(2,1)S(1)} %get-tuple-element.63), channel_id=1, source_target_pairs={{1,2},{3,4},{5,6},{7,8},{9,10},{11,12},{13,14},{15,16},{17,18},{19... | collective-permute-start | bytes 221192 | tf_op jit(solution)/shard_map/ppermute | solution.py:363
  82.0 4.4 %collective-permute-done.11.far_part = bf16[96,384]{1,0:T(8,128)(2,1)S(1)} collective-permute-done((bf16[96,384]{1,0:T(8,128)(2,1)S(1)}, bf16[96,384]{1,0:T(8,128)(2,1)S(1)}, u32[]{:S(2)}, u32[]{:S(2)}) %collective-permute-start.11) | collective-permute-done | bytes 73760 | tf_op jit(solution)/shard_map/ppermute | solution.py:363
  87.0 5.6 %all-to-all-start.1 = ((bf16[4,192,384]{2,1,0:T(8,128)(2,1)}), bf16[4,192,384]{2,1,0:T(8,128)(2,1)S(1)}, u32[]{:S(2)}, u32[]{:S(2)}) async-start(bf16[4,192,384]{2,1,0:T(8,128)(2,1)} %get-tuple-element.67), calls=%async_computation.1 | async-start | bytes 1179648 | tf_op jit(solution)/shard_map/all_to_all | solution.py:544
  92.6 4.1 %collective-permute-start.13 = (f32[1,4,1536]{2,1,0:T(4,128)S(1)}, f32[1,4,1536]{2,1,0:T(4,128)S(1)}, u32[]{:S(2)}, u32[]{:S(2)}) collective-permute-start(f32[1,4,1536]{2,1,0:T(4,128)S(1)} %get-tuple-element.68.own), channel_id=1, source_target_pairs={{0,2},{1,3},{2,0},{3,1},{4,6},{5,7},{6,4},{7,5},{8,10},{9,11},{10,... | collective-permute-start | bytes 73736 | tf_op jit(solution)/shard_map/ppermute | solution.py:405
  96.7 0.9 collective-permute-done.15.refs_2_
  99.0 4.0 %collective-permute-start.16 = (f32[1,4,1536]{2,1,0:T(4,128)S(1)}, f32[1,4,1536]{2,1,0:T(4,128)S(1)}, u32[]{:S(2)}, u32[]{:S(2)}) collective-permute-start(f32[1,4,1536]{2,1,0:T(4,128)S(1)} %add_group.1.mods), channel_id=1, source_target_pairs={{0,8},{1,9},{2,10},{3,11},{4,12},{5,13},{6,14},{7,15},{8,0},{9,1},... | collective-permute-start | bytes 73736 | tf_op jit(solution)/shard_map/ppermute | solution.py:405
  103.0 0.9 collective-permute-done.18.refs_2_
  105.0 2.6 %all-to-all-done.1.received = bf16[4,192,384]{2,1,0:T(8,128)(2,1)S(1)} async-done(((bf16[4,192,384]{2,1,0:T(8,128)(2,1)}), bf16[4,192,384]{2,1,0:T(8,128)(2,1)S(1)}, u32[]{:S(2)}, u32[]{:S(2)}) %all-to-all-start.1) | async-done | bytes 589856 | tf_op jit(solution)/shard_map/all_to_all | solution.py:544
  107.6 0.9 finish.1
  (36 shorter events, 5.3 us)
Async XLA Ops:
  0.6 12.5 %copy-start.4 = (f32[1,4,1536]{2,1,0:T(4,128)S(1)}, f32[1,4,1536]{2,1,0:T(4,128)}, u32[]{:S(2)}) copy-start(f32[1,4,1536]{2,1,0:T(4,128)} %refs_2_.3) | copy-start | bytes 73732
  0.6 12.5 %copy-start.1 = (bf16[1,2,32,1536]{3,2,1,0:T(8,128)(2,1)S(1)}, bf16[1,2,32,1536]{3,2,1,0:T(8,128)(2,1)}, u32[]{:S(2)}) copy-start(bf16[1,2,32,1536]{3,2,1,0:T(8,128)(2,1)} %refs_1_.3) | copy-start | bytes 589828
  0.7 12.5 %copy-start = (bf16[1,2,64,1536]{3,2,1,0:T(8,128)(2,1)S(1)}, bf16[1,2,64,1536]{3,2,1,0:T(8,128)(2,1)}, u32[]{:S(2)}) copy-start(bf16[1,2,64,1536]{3,2,1,0:T(8,128)(2,1)} %refs_0_.3) | copy-start | bytes 1179652
  2.7 14.5 %collective-permute-start = (bf16[208,384]{1,0:T(8,128)(2,1)}, bf16[208,384]{1,0:T(8,128)(2,1)S(1)}, u32[]{:S(2)}, u32[]{:S(2)}) collective-permute-start(bf16[208,384]{1,0:T(8,128)(2,1)} %get-tuple-element.36), channel_id=1, source_target_pairs={{0,64},{64,128},{128,192},{192,0},{1,65},{65,129},{129,193},{193,1... | collective-permute-start | bytes 479240 | tf_op jit(solution)/shard_map/ppermute | solution.py:378
  6.0 7.2 %copy-start.5 = (s32[1,2]{1,0:T(1,128)S(1)}, s32[1,2]{1,0:T(1,128)}, u32[]{:S(2)}) copy-start(s32[1,2]{1,0:T(1,128)} %refs_3_.3) | copy-start | bytes 28
  6.0 7.2 %copy-start.6 = (s32[1,2]{1,0:T(1,128)S(1)}, s32[1,2]{1,0:T(1,128)}, u32[]{:S(2)}) copy-start(s32[1,2]{1,0:T(1,128)} %refs_4_.3) | copy-start | bytes 28
  6.0 11.2 %collective-permute-start.1 = (bf16[208,384]{1,0:T(8,128)(2,1)}, bf16[208,384]{1,0:T(8,128)(2,1)S(1)}, u32[]{:S(2)}, u32[]{:S(2)}) collective-permute-start(bf16[208,384]{1,0:T(8,128)(2,1)} %get-tuple-element.37), channel_id=1, source_target_pairs={{0,192},{64,0},{128,64},{192,128},{1,193},{65,1},{129,65},{193,129... | collective-permute-start | bytes 479240 | tf_op jit(solution)/shard_map/ppermute | solution.py:378
  8.3 18.4 %collective-permute-start.2 = (bf16[208,384]{1,0:T(8,128)(2,1)}, bf16[208,384]{1,0:T(8,128)(2,1)S(1)}, u32[]{:S(2)}, u32[]{:S(2)}) collective-permute-start(bf16[208,384]{1,0:T(8,128)(2,1)} %get-tuple-element.38), channel_id=1, source_target_pairs={{0,128},{64,192},{128,0},{192,64},{1,129},{65,193},{129,1},{193,65... | collective-permute-start | bytes 479240 | tf_op jit(solution)/shard_map/ppermute | solution.py:378
  13.2 1.0 copy-start.2
  14.2 0.9 copy-start.3
  26.7 12.3 %collective-permute-start.3 = (bf16[4,96,384]{2,1,0:T(8,128)(2,1)S(1)}, bf16[4,96,384]{2,1,0:T(8,128)(2,1)S(1)}, u32[]{:S(2)}, u32[]{:S(2)}) collective-permute-start(bf16[4,96,384]{2,1,0:T(8,128)(2,1)S(1)} %get-tuple-element.40.far_own.refs_0_), channel_id=1, source_target_pairs={{1,2},{3,4},{5,6},{7,8},{9,10},{11,12},{13,14},{15,16},{17,18},{19... | collective-permute-start | bytes 884744 | tf_op jit(solution)/shard_map/ppermute | solution.py:363
  28.6 10.3 %collective-permute-start.4 = (bf16[4,96,384]{2,1,0:T(8,128)(2,1)S(1)}, bf16[4,96,384]{2,1,0:T(8,128)(2,1)S(1)}, u32[]{:S(2)}, u32[]{:S(2)}) collective-permute-start(bf16[4,96,384]{2,1,0:T(8,128)(2,1)S(1)} %get-tuple-element.41.near_own.refs_1_), channel_id=1, source_target_pairs={{0,1},{2,3},{4,5},{6,7},{8,9},{10,11},{12,13},{14,15},{16,17},{18,... | collective-permute-start | bytes 884744 | tf_op jit(solution)/shard_map/ppermute | solution.py:363
  40.0 9.9 %collective-permute-start.5 = (bf16[96,384]{1,0:T(8,128)(2,1)S(1)}, bf16[96,384]{1,0:T(8,128)(2,1)S(1)}, u32[]{:S(2)}, u32[]{:S(2)}) collective-permute-start(bf16[96,384]{1,0:T(8,128)(2,1)S(1)} %get-tuple-element.45), channel_id=1, source_target_pairs={{1,2},{3,4},{5,6},{7,8},{9,10},{11,12},{13,14},{15,16},{17,18},{19... | collective-permute-start | bytes 221192 | tf_op jit(solution)/shard_map/ppermute | solution.py:363
  41.9 8.0 %collective-permute-start.6 = (bf16[96,384]{1,0:T(8,128)(2,1)S(1)}, bf16[96,384]{1,0:T(8,128)(2,1)S(1)}, u32[]{:S(2)}, u32[]{:S(2)}) collective-permute-start(bf16[96,384]{1,0:T(8,128)(2,1)S(1)} %get-tuple-element.46), channel_id=1, source_target_pairs={{0,1},{2,3},{4,5},{6,7},{8,9},{10,11},{12,13},{14,15},{16,17},{18,... | collective-permute-start | bytes 221192 | tf_op jit(solution)/shard_map/ppermute | solution.py:363
  50.7 9.9 %collective-permute-start.7 = (bf16[96,384]{1,0:T(8,128)(2,1)S(1)}, bf16[96,384]{1,0:T(8,128)(2,1)S(1)}, u32[]{:S(2)}, u32[]{:S(2)}) collective-permute-start(bf16[96,384]{1,0:T(8,128)(2,1)S(1)} %get-tuple-element.51), channel_id=1, source_target_pairs={{1,2},{3,4},{5,6},{7,8},{9,10},{11,12},{13,14},{15,16},{17,18},{19... | collective-permute-start | bytes 221192 | tf_op jit(solution)/shard_map/ppermute | solution.py:363
  52.6 8.0 %collective-permute-start.8 = (bf16[96,384]{1,0:T(8,128)(2,1)S(1)}, bf16[96,384]{1,0:T(8,128)(2,1)S(1)}, u32[]{:S(2)}, u32[]{:S(2)}) collective-permute-start(bf16[96,384]{1,0:T(8,128)(2,1)S(1)} %get-tuple-element.52), channel_id=1, source_target_pairs={{0,1},{2,3},{4,5},{6,7},{8,9},{10,11},{12,13},{14,15},{16,17},{18,... | collective-permute-start | bytes 221192 | tf_op jit(solution)/shard_map/ppermute | solution.py:363
  61.4 9.9 %collective-permute-start.9 = (bf16[96,384]{1,0:T(8,128)(2,1)S(1)}, bf16[96,384]{1,0:T(8,128)(2,1)S(1)}, u32[]{:S(2)}, u32[]{:S(2)}) collective-permute-start(bf16[96,384]{1,0:T(8,128)(2,1)S(1)} %get-tuple-element.55), channel_id=1, source_target_pairs={{1,2},{3,4},{5,6},{7,8},{9,10},{11,12},{13,14},{15,16},{17,18},{19... | collective-permute-start | bytes 221192 | tf_op jit(solution)/shard_map/ppermute | solution.py:363
  63.3 8.0 %collective-permute-start.10 = (bf16[96,384]{1,0:T(8,128)(2,1)S(1)}, bf16[96,384]{1,0:T(8,128)(2,1)S(1)}, u32[]{:S(2)}, u32[]{:S(2)}) collective-permute-start(bf16[96,384]{1,0:T(8,128)(2,1)S(1)} %get-tuple-element.56), channel_id=1, source_target_pairs={{0,1},{2,3},{4,5},{6,7},{8,9},{10,11},{12,13},{14,15},{16,17},{18,... | collective-permute-start | bytes 221192 | tf_op jit(solution)/shard_map/ppermute | solution.py:363
  72.6 13.7 %all-to-all-start = ((f32[16,4,384]{2,1,0:T(4,128)}), f32[16,4,384]{2,1,0:T(4,128)S(1)}, u32[]{:S(2)}, u32[]{:S(2)}) async-start(f32[16,4,384]{2,1,0:T(4,128)} %get-tuple-element.66), calls=%async_computation | async-start | bytes 196608 | tf_op jit(solution)/shard_map/all_to_all | solution.py:395
  76.3 10.0 %collective-permute-start.11 = (bf16[96,384]{1,0:T(8,128)(2,1)S(1)}, bf16[96,384]{1,0:T(8,128)(2,1)S(1)}, u32[]{:S(2)}, u32[]{:S(2)}) collective-permute-start(bf16[96,384]{1,0:T(8,128)(2,1)S(1)} %get-tuple-element.63), channel_id=1, source_target_pairs={{1,2},{3,4},{5,6},{7,8},{9,10},{11,12},{13,14},{15,16},{17,18},{19... | collective-permute-start | bytes 221192 | tf_op jit(solution)/shard_map/ppermute | solution.py:363
  81.9 4.5 %collective-permute-start.12 = (bf16[96,384]{1,0:T(8,128)(2,1)S(1)}, bf16[96,384]{1,0:T(8,128)(2,1)S(1)}, u32[]{:S(2)}, u32[]{:S(2)}) collective-permute-start(bf16[96,384]{1,0:T(8,128)(2,1)S(1)} %get-tuple-element.64), channel_id=1, source_target_pairs={{0,1},{2,3},{4,5},{6,7},{8,9},{10,11},{12,13},{14,15},{16,17},{18,... | collective-permute-start | bytes 221192 | tf_op jit(solution)/shard_map/ppermute | solution.py:363
  87.0 20.6 %all-to-all-start.1 = ((bf16[4,192,384]{2,1,0:T(8,128)(2,1)}), bf16[4,192,384]{2,1,0:T(8,128)(2,1)S(1)}, u32[]{:S(2)}, u32[]{:S(2)}) async-start(bf16[4,192,384]{2,1,0:T(8,128)(2,1)} %get-tuple-element.67), calls=%async_computation.1 | async-start | bytes 1179648 | tf_op jit(solution)/shard_map/all_to_all | solution.py:544
  92.6 5.0 %collective-permute-start.15 = (f32[1,4,1536]{2,1,0:T(4,128)S(1)}, f32[1,4,1536]{2,1,0:T(4,128)S(1)}, u32[]{:S(2)}, u32[]{:S(2)}) collective-permute-start(f32[1,4,1536]{2,1,0:T(4,128)S(1)} %get-tuple-element.68.own), channel_id=1, source_target_pairs={{0,6},{1,7},{2,4},{3,5},{4,2},{5,3},{6,0},{7,1},{8,14},{9,15},{10,... | collective-permute-start | bytes 73736 | tf_op jit(solution)/shard_map/ppermute | solution.py:405
  92.6 5.3 %collective-permute-start.14 = (f32[1,4,1536]{2,1,0:T(4,128)S(1)}, f32[1,4,1536]{2,1,0:T(4,128)S(1)}, u32[]{:S(2)}, u32[]{:S(2)}) collective-permute-start(f32[1,4,1536]{2,1,0:T(4,128)S(1)} %get-tuple-element.68.own), channel_id=1, source_target_pairs={{0,4},{1,5},{2,6},{3,7},{4,0},{5,1},{6,2},{7,3},{8,12},{9,13},{10,... | collective-permute-start | bytes 73736 | tf_op jit(solution)/shard_map/ppermute | solution.py:405
  92.6 6.1 %collective-permute-start.13 = (f32[1,4,1536]{2,1,0:T(4,128)S(1)}, f32[1,4,1536]{2,1,0:T(4,128)S(1)}, u32[]{:S(2)}, u32[]{:S(2)}) collective-permute-start(f32[1,4,1536]{2,1,0:T(4,128)S(1)} %get-tuple-element.68.own), channel_id=1, source_target_pairs={{0,2},{1,3},{2,0},{3,1},{4,6},{5,7},{6,4},{7,5},{8,10},{9,11},{10,... | collective-permute-start | bytes 73736 | tf_op jit(solution)/shard_map/ppermute | solution.py:405
  98.8 5.1 %collective-permute-start.18 = (f32[1,4,1536]{2,1,0:T(4,128)S(1)}, f32[1,4,1536]{2,1,0:T(4,128)S(1)}, u32[]{:S(2)}, u32[]{:S(2)}) collective-permute-start(f32[1,4,1536]{2,1,0:T(4,128)S(1)} %add_group.1.mods), channel_id=1, source_target_pairs={{0,24},{1,25},{2,26},{3,27},{4,28},{5,29},{6,30},{7,31},{8,16},{9,... | collective-permute-start | bytes 73736 | tf_op jit(solution)/shard_map/ppermute | solution.py:405
  98.9 5.4 %collective-permute-start.17 = (f32[1,4,1536]{2,1,0:T(4,128)S(1)}, f32[1,4,1536]{2,1,0:T(4,128)S(1)}, u32[]{:S(2)}, u32[]{:S(2)}) collective-permute-start(f32[1,4,1536]{2,1,0:T(4,128)S(1)} %add_group.1.mods), channel_id=1, source_target_pairs={{0,16},{1,17},{2,18},{3,19},{4,20},{5,21},{6,22},{7,23},{8,24},{9,... | collective-permute-start | bytes 73736 | tf_op jit(solution)/shard_map/ppermute | solution.py:405
  99.0 6.0 %collective-permute-start.16 = (f32[1,4,1536]{2,1,0:T(4,128)S(1)}, f32[1,4,1536]{2,1,0:T(4,128)S(1)}, u32[]{:S(2)}, u32[]{:S(2)}) collective-permute-start(f32[1,4,1536]{2,1,0:T(4,128)S(1)} %add_group.1.mods), channel_id=1, source_target_pairs={{0,8},{1,9},{2,10},{3,11},{4,12},{5,13},{6,14},{7,15},{8,0},{9,1},... | collective-permute-start | bytes 73736 | tf_op jit(solution)/shard_map/ppermute | solution.py:405

commit v3 on v2

--- a/solution.py
+++ b/solution.py
@@ -188,10 +188,13 @@
         split(jnp.concatenate([unit[0], unit[0] * (by - mean)], axis=0))
         for by, mean, unit in zip(by_weights, means, units)
     ]
-    outs = [dot_rows(both, unit[3], ((1,), (0,))) for both, unit in zip(boths, units)]
+    outs = []
+    for (high, low), unit in zip(boths, units):
+        count = unit[1].shape[0]
+        out = dot(jnp.concatenate([high, low[count:]], axis=0), unit[3], ((1,), (0,)))
+        outs.append((out[:count], out[count : 2 * count] + out[2 * count :]))
     found = []
     for grad, both, out, (_, cot, own, _, scale, _) in zip(grads, boths, outs, units):
-        count = cot.shape[0]
         own32 = own.astype(F32)
         scaled = split(own32 * scale)
         high, low = (jnp.concatenate([g, q], axis=0) for g, q in zip(grad, scaled))
@@ -200,7 +203,7 @@
             jnp.concatenate([high, high, low], axis=0),
             ((0,), (0,)),
         )
-        mixed, back = out[:count], out[count:]
+        mixed, back = out
         by_scale = jnp.sum(own32 * back, axis=0, keepdims=True) * SCALE
         by_gate = jnp.sum(cot * mixed, axis=0, keepdims=True)
         found.append((back * scale, by_context, by_scale, by_gate))

time: 109 us -> 109 us (level)
  no operation moved by 1% of the time
where the time goes in v3:
time: 109 us; the launch traced here: 108 us
  waiting for transfers between devices  51.3 us (47%)
  starting transfers between devices  43.5 us (40%)
  Pallas kernels  10.9 us (10%)
  local copies, waits for them, and re-layouts  1.94 us (2%)
    ppermute x10, waiting for transfers between devices, swap(): return lax.ppermute(value, 'seq', pairs + [(b, a) for a, b in pairs])  34.2 us
    ppermute x10, starting transfers between devices, swap(): return lax.ppermute(value, 'seq', pairs + [(b, a) for a, b in pairs])  15.4 us
    ppermute x3, starting transfers between devices, to_section(): lax.ppermute(value, 'section', [(s, (s + k) % count) for s in range(count)])  10.5 us
    ppermute x3, waiting for transfers between devices, to_section(): lax.ppermute(value, 'section', [(s, (s + k) % count) for s in range(count)])  10.4 us
    ppermute x6, starting transfers between devices, group_moves(): lax.ppermute(value, 'seq', [(i, i ^ mask) for i in range(count)])  8.26 us
    all_to_all x1, starting transfers between devices, local(): received = lax.all_to_all(out, 'section', 0, 0, tiled=True)  5.61 us
    pallas_call x7, Pallas kernels, run(): call(body, tuple(outs), grid=(1,), in_specs=specs or like(arrays), out_sp...  4.34 us
    ppermute x6, waiting for transfers between devices, group_moves(): lax.ppermute(value, 'seq', [(i, i ^ mask) for i in range(count)])  4.12 us
  transfers between devices with their start and end apart: 21, of which 14 were waited for; matrix products, arithmetic and copies ran while one was open for 0% of the time, Pallas kernels for 3%

profile of v3, /device:TPU:32, one launch (start us, length us, event | category | flops | bytes accessed | tf_op | source)
XLA Modules:
  0.0 108.3 jit_solution(7840627292482956635)
XLA Ops:
  0.7 2.0 %prepare.1 = (bf16[208,384]{1,0:T(8,128)(2,1)}, bf16[208,384]{1,0:T(8,128)(2,1)}, bf16[208,384]{1,0:T(8,128)(2,1)}) custom-call(bf16[1,2,64,1536]{3,2,1,0:T(8,128)(2,1)} %refs_0_.3, bf16[1,2,32,1536]{3,2,1,0:T(8,128)(2,1)} %refs_1_.3, f32[1,4,1536]{2,1,0:T(4,128)} %refs_2_.3, s32[1,2]{1,0:T(1,128)} %refs_3_.3, s32[1,2]{1,0:T(1,128)} %refs_4_.3), custom_call_target="tpu_custom_call" | custom-call | bytes 1048576 | tf_op jit(solution)/shard_map/prepare/pallas_call | solution.py:436
  2.7 3.3 %collective-permute-start = (bf16[208,384]{1,0:T(8,128)(2,1)}, bf16[208,384]{1,0:T(8,128)(2,1)S(1)}, u32[]{:S(2)}, u32[]{:S(2)}) collective-permute-start(bf16[208,384]{1,0:T(8,128)(2,1)} %get-tuple-element.36), channel_id=1, source_target_pairs={{0,64},{64,128},{128,192},{192,0},{1,65},{65,129},{129,193},{193,1... | collective-permute-start | bytes 479240 | tf_op jit(solution)/shard_map/ppermute | solution.py:381
  6.0 2.2 %collective-permute-start.1 = (bf16[208,384]{1,0:T(8,128)(2,1)}, bf16[208,384]{1,0:T(8,128)(2,1)S(1)}, u32[]{:S(2)}, u32[]{:S(2)}) collective-permute-start(bf16[208,384]{1,0:T(8,128)(2,1)} %get-tuple-element.37), channel_id=1, source_target_pairs={{0,192},{64,0},{128,64},{192,128},{1,193},{65,1},{129,65},{193,129... | collective-permute-start | bytes 479240 | tf_op jit(solution)/shard_map/ppermute | solution.py:381
  8.3 4.9 %collective-permute-start.2 = (bf16[208,384]{1,0:T(8,128)(2,1)}, bf16[208,384]{1,0:T(8,128)(2,1)S(1)}, u32[]{:S(2)}, u32[]{:S(2)}) collective-permute-start(bf16[208,384]{1,0:T(8,128)(2,1)} %get-tuple-element.38), channel_id=1, source_target_pairs={{0,128},{64,192},{128,0},{192,64},{1,129},{65,193},{129,1},{193,65... | collective-permute-start | bytes 479240 | tf_op jit(solution)/shard_map/ppermute | solution.py:381
  13.2 1.0 copy-done.2
  14.2 0.9 copy-done.3
  15.1 1.1 %prepare_own.1 = (bf16[208,384]{1,0:T(8,128)(2,1)S(1)}, bf16[192,384]{1,0:T(8,128)(2,1)S(1)}) custom-call(bf16[1,2,64,1536]{3,2,1,0:T(8,128)(2,1)S(1)} %copy-done, bf16[1,2,32,1536]{3,2,1,0:T(8,128)(2,1)S(1)} %copy-done.1, f32[1,4,1536]{2,1,0:T(4,128)S(1)} %copy-done.4, s32[1,2]{1,0:T(1,128)S(1)} %copy-done.5, s32[1,2]{1,0:T(1,128)S(1)} %copy-done.6, ...), custom_call_target="tpu_custom_call" | custom-call | bytes 1048576 | tf_op jit(solution)/shard_map/prepare_own/pallas_call | solution.py:436
  16.3 0.9 collective-permute-done.refs_0_
  17.2 9.5 %collective-permute-done.2.refs_2_ = bf16[208,384]{1,0:T(8,128)(2,1)S(1)} collective-permute-done((bf16[208,384]{1,0:T(8,128)(2,1)}, bf16[208,384]{1,0:T(8,128)(2,1)S(1)}, u32[]{:S(2)}, u32[]{:S(2)}) %collective-permute-start.2) | collective-permute-done | bytes 159776 | tf_op jit(solution)/shard_map/ppermute | solution.py:381
  26.7 1.9 %collective-permute-start.3 = (bf16[4,96,384]{2,1,0:T(8,128)(2,1)S(1)}, bf16[4,96,384]{2,1,0:T(8,128)(2,1)S(1)}, u32[]{:S(2)}, u32[]{:S(2)}) collective-permute-start(bf16[4,96,384]{2,1,0:T(8,128)(2,1)S(1)} %get-tuple-element.40.far_own.refs_0_), channel_id=1, source_target_pairs={{1,2},{3,4},{5,6},{7,8},{9,10},{11,12},{13,14},{15,16},{17,18},{19... | collective-permute-start | bytes 884744 | tf_op jit(solution)/shard_map/ppermute | solution.py:366
  28.6 1.8 %collective-permute-start.4 = (bf16[4,96,384]{2,1,0:T(8,128)(2,1)S(1)}, bf16[4,96,384]{2,1,0:T(8,128)(2,1)S(1)}, u32[]{:S(2)}, u32[]{:S(2)}) collective-permute-start(bf16[4,96,384]{2,1,0:T(8,128)(2,1)S(1)} %get-tuple-element.41.near_own.refs_1_), channel_id=1, source_target_pairs={{0,1},{2,3},{4,5},{6,7},{8,9},{10,11},{12,13},{14,15},{16,17},{18,... | collective-permute-start | bytes 884744 | tf_op jit(solution)/shard_map/ppermute | solution.py:366
  30.4 8.6 %collective-permute-done.3.far_in.refs_2_ = bf16[4,96,384]{2,1,0:T(8,128)(2,1)S(1)} collective-permute-done((bf16[4,96,384]{2,1,0:T(8,128)(2,1)S(1)}, bf16[4,96,384]{2,1,0:T(8,128)(2,1)S(1)}, u32[]{:S(2)}, u32[]{:S(2)}) %collective-permute-start.3) | collective-permute-done | bytes 294944 | tf_op jit(solution)/shard_map/ppermute | solution.py:366
  39.0 1.0 top_layer.1
  39.9 1.9 %collective-permute-start.5 = (bf16[96,384]{1,0:T(8,128)(2,1)S(1)}, bf16[96,384]{1,0:T(8,128)(2,1)S(1)}, u32[]{:S(2)}, u32[]{:S(2)}) collective-permute-start(bf16[96,384]{1,0:T(8,128)(2,1)S(1)} %get-tuple-element.45), channel_id=1, source_target_pairs={{1,2},{3,4},{5,6},{7,8},{9,10},{11,12},{13,14},{15,16},{17,18},{19... | collective-permute-start | bytes 221192 | tf_op jit(solution)/shard_map/ppermute | solution.py:366
  42.0 1.5 %weights_ahead.1 = (f32[3,2,3,64,64]{4,3,2,1,0:T(8,128)S(1)}, f32[3,2,3,32,128]{4,3,2,1,0:T(8,128)S(1)}) custom-call(bf16[4,96,384]{2,1,0:T(8,128)(2,1)S(1)} %get-tuple-element.40.far_own.refs_0_, bf16[4,96,384]{2,1,0:T(8,128)(2,1)S(1)} %get-tuple-element.41.near_own.refs_1_, bf16[4,96,384]{2,1,0:T(8,128)(2,1)S(1)} %collective-permute-done.3.far_in.refs_2_, ...), custom_call_target="tpu_custom_call" | custom-call | flops 600000000 | bytes 1048576 | tf_op jit(solution)/shard_map/weights_ahead/pallas_call | solution.py:488
  43.4 6.4 %collective-permute-done.5.refs_6_ = bf16[96,384]{1,0:T(8,128)(2,1)S(1)} collective-permute-done((bf16[96,384]{1,0:T(8,128)(2,1)S(1)}, bf16[96,384]{1,0:T(8,128)(2,1)S(1)}, u32[]{:S(2)}, u32[]{:S(2)}) %collective-permute-start.5) | collective-permute-done | bytes 73760 | tf_op jit(solution)/shard_map/ppermute | solution.py:366
  50.6 1.9 %collective-permute-start.7 = (bf16[96,384]{1,0:T(8,128)(2,1)S(1)}, bf16[96,384]{1,0:T(8,128)(2,1)S(1)}, u32[]{:S(2)}, u32[]{:S(2)}) collective-permute-start(bf16[96,384]{1,0:T(8,128)(2,1)S(1)} %get-tuple-element.51), channel_id=1, source_target_pairs={{1,2},{3,4},{5,6},{7,8},{9,10},{11,12},{13,14},{15,16},{17,18},{19... | collective-permute-start | bytes 221192 | tf_op jit(solution)/shard_map/ppermute | solution.py:366
  52.7 7.9 %collective-permute-done.7.refs_6_ = bf16[96,384]{1,0:T(8,128)(2,1)S(1)} collective-permute-done((bf16[96,384]{1,0:T(8,128)(2,1)S(1)}, bf16[96,384]{1,0:T(8,128)(2,1)S(1)}, u32[]{:S(2)}, u32[]{:S(2)}) %collective-permute-start.7) | collective-permute-done | bytes 73760 | tf_op jit(solution)/shard_map/ppermute | solution.py:366
  61.3 1.9 %collective-permute-start.9 = (bf16[96,384]{1,0:T(8,128)(2,1)S(1)}, bf16[96,384]{1,0:T(8,128)(2,1)S(1)}, u32[]{:S(2)}, u32[]{:S(2)}) collective-permute-start(bf16[96,384]{1,0:T(8,128)(2,1)S(1)} %get-tuple-element.55), channel_id=1, source_target_pairs={{1,2},{3,4},{5,6},{7,8},{9,10},{11,12},{13,14},{15,16},{17,18},{19... | collective-permute-start | bytes 221192 | tf_op jit(solution)/shard_map/ppermute | solution.py:366
  63.3 0.9 ahead.1
  64.2 7.0 %collective-permute-done.9.refs_6_ = bf16[96,384]{1,0:T(8,128)(2,1)S(1)} collective-permute-done((bf16[96,384]{1,0:T(8,128)(2,1)S(1)}, bf16[96,384]{1,0:T(8,128)(2,1)S(1)}, u32[]{:S(2)}, u32[]{:S(2)}) %collective-permute-start.9) | collective-permute-done | bytes 73760 | tf_op jit(solution)/shard_map/ppermute | solution.py:366
  71.2 1.2 %last_layer.1 = (bf16[4,192,384]{2,1,0:T(8,128)(2,1)}, f32[16,4,384]{2,1,0:T(4,128)}, f32[192,384]{1,0:T(8,128)S(1)}, bf16[96,384]{1,0:T(8,128)(2,1)S(1)}, bf16[96,384]{1,0:T(8,128)(2,1)S(1)}) custom-call(bf16[4,96,384]{2,1,0:T(8,128)(2,1)S(1)} %get-tuple-element.40.far_own.refs_0_, ...), custom_call_target="tpu_custom_call", output_to_operand_aliasing={{0}: (10, {}), {1}: (11, {})} | custom-call | flops 200000000 | bytes 1048576 | tf_op jit(solution)/shard_map/last_layer/pallas_call | solution.py:525
  72.4 3.7 %all-to-all-start = ((f32[16,4,384]{2,1,0:T(4,128)}), f32[16,4,384]{2,1,0:T(4,128)S(1)}, u32[]{:S(2)}, u32[]{:S(2)}) async-start(f32[16,4,384]{2,1,0:T(4,128)} %get-tuple-element.66), calls=%async_computation | async-start | bytes 196608 | tf_op jit(solution)/shard_map/all_to_all | solution.py:398
  76.1 5.6 %collective-permute-start.11 = (bf16[96,384]{1,0:T(8,128)(2,1)S(1)}, bf16[96,384]{1,0:T(8,128)(2,1)S(1)}, u32[]{:S(2)}, u32[]{:S(2)}) collective-permute-start(bf16[96,384]{1,0:T(8,128)(2,1)S(1)} %get-tuple-element.63), channel_id=1, source_target_pairs={{1,2},{3,4},{5,6},{7,8},{9,10},{11,12},{13,14},{15,16},{17,18},{19... | collective-permute-start | bytes 221192 | tf_op jit(solution)/shard_map/ppermute | solution.py:366
  81.8 4.3 %collective-permute-done.11.far_part = bf16[96,384]{1,0:T(8,128)(2,1)S(1)} collective-permute-done((bf16[96,384]{1,0:T(8,128)(2,1)S(1)}, bf16[96,384]{1,0:T(8,128)(2,1)S(1)}, u32[]{:S(2)}, u32[]{:S(2)}) %collective-permute-start.11) | collective-permute-done | bytes 73760 | tf_op jit(solution)/shard_map/ppermute | solution.py:366
  86.8 5.6 %all-to-all-start.1 = ((bf16[4,192,384]{2,1,0:T(8,128)(2,1)}), bf16[4,192,384]{2,1,0:T(8,128)(2,1)S(1)}, u32[]{:S(2)}, u32[]{:S(2)}) async-start(bf16[4,192,384]{2,1,0:T(8,128)(2,1)} %get-tuple-element.67), calls=%async_computation.1 | async-start | bytes 1179648 | tf_op jit(solution)/shard_map/all_to_all | solution.py:547
  92.5 4.1 %collective-permute-start.13 = (f32[1,4,1536]{2,1,0:T(4,128)S(1)}, f32[1,4,1536]{2,1,0:T(4,128)S(1)}, u32[]{:S(2)}, u32[]{:S(2)}) collective-permute-start(f32[1,4,1536]{2,1,0:T(4,128)S(1)} %get-tuple-element.68.own), channel_id=1, source_target_pairs={{0,2},{1,3},{2,0},{3,1},{4,6},{5,7},{6,4},{7,5},{8,10},{9,11},{10,... | collective-permute-start | bytes 73736 | tf_op jit(solution)/shard_map/ppermute | solution.py:408
  96.6 0.9 collective-permute-done.15.refs_2_
  98.8 4.0 %collective-permute-start.16 = (f32[1,4,1536]{2,1,0:T(4,128)S(1)}, f32[1,4,1536]{2,1,0:T(4,128)S(1)}, u32[]{:S(2)}, u32[]{:S(2)}) collective-permute-start(f32[1,4,1536]{2,1,0:T(4,128)S(1)} %add_group.1.mods), channel_id=1, source_target_pairs={{0,8},{1,9},{2,10},{3,11},{4,12},{5,13},{6,14},{7,15},{8,0},{9,1},... | collective-permute-start | bytes 73736 | tf_op jit(solution)/shard_map/ppermute | solution.py:408
  102.8 0.9 collective-permute-done.18.refs_2_
  104.9 2.6 %all-to-all-done.1.received = bf16[4,192,384]{2,1,0:T(8,128)(2,1)S(1)} async-done(((bf16[4,192,384]{2,1,0:T(8,128)(2,1)}), bf16[4,192,384]{2,1,0:T(8,128)(2,1)S(1)}, u32[]{:S(2)}, u32[]{:S(2)}) %all-to-all-start.1) | async-done | bytes 589856 | tf_op jit(solution)/shard_map/all_to_all | solution.py:547
  107.5 0.9 finish.1
  (36 shorter events, 5.2 us)
Async XLA Ops:
  0.6 12.5 %copy-start.4 = (f32[1,4,1536]{2,1,0:T(4,128)S(1)}, f32[1,4,1536]{2,1,0:T(4,128)}, u32[]{:S(2)}) copy-start(f32[1,4,1536]{2,1,0:T(4,128)} %refs_2_.3) | copy-start | bytes 73732
  0.6 12.5 %copy-start.1 = (bf16[1,2,32,1536]{3,2,1,0:T(8,128)(2,1)S(1)}, bf16[1,2,32,1536]{3,2,1,0:T(8,128)(2,1)}, u32[]{:S(2)}) copy-start(bf16[1,2,32,1536]{3,2,1,0:T(8,128)(2,1)} %refs_1_.3) | copy-start | bytes 589828
  0.7 12.5 %copy-start = (bf16[1,2,64,1536]{3,2,1,0:T(8,128)(2,1)S(1)}, bf16[1,2,64,1536]{3,2,1,0:T(8,128)(2,1)}, u32[]{:S(2)}) copy-start(bf16[1,2,64,1536]{3,2,1,0:T(8,128)(2,1)} %refs_0_.3) | copy-start | bytes 1179652
  2.7 14.5 %collective-permute-start = (bf16[208,384]{1,0:T(8,128)(2,1)}, bf16[208,384]{1,0:T(8,128)(2,1)S(1)}, u32[]{:S(2)}, u32[]{:S(2)}) collective-permute-start(bf16[208,384]{1,0:T(8,128)(2,1)} %get-tuple-element.36), channel_id=1, source_target_pairs={{0,64},{64,128},{128,192},{192,0},{1,65},{65,129},{129,193},{193,1... | collective-permute-start | bytes 479240 | tf_op jit(solution)/shard_map/ppermute | solution.py:381
  6.0 7.2 %copy-start.5 = (s32[1,2]{1,0:T(1,128)S(1)}, s32[1,2]{1,0:T(1,128)}, u32[]{:S(2)}) copy-start(s32[1,2]{1,0:T(1,128)} %refs_3_.3) | copy-start | bytes 28
  6.0 7.2 %copy-start.6 = (s32[1,2]{1,0:T(1,128)S(1)}, s32[1,2]{1,0:T(1,128)}, u32[]{:S(2)}) copy-start(s32[1,2]{1,0:T(1,128)} %refs_4_.3) | copy-start | bytes 28
  6.0 11.2 %collective-permute-start.1 = (bf16[208,384]{1,0:T(8,128)(2,1)}, bf16[208,384]{1,0:T(8,128)(2,1)S(1)}, u32[]{:S(2)}, u32[]{:S(2)}) collective-permute-start(bf16[208,384]{1,0:T(8,128)(2,1)} %get-tuple-element.37), channel_id=1, source_target_pairs={{0,192},{64,0},{128,64},{192,128},{1,193},{65,1},{129,65},{193,129... | collective-permute-start | bytes 479240 | tf_op jit(solution)/shard_map/ppermute | solution.py:381
  8.3 18.4 %collective-permute-start.2 = (bf16[208,384]{1,0:T(8,128)(2,1)}, bf16[208,384]{1,0:T(8,128)(2,1)S(1)}, u32[]{:S(2)}, u32[]{:S(2)}) collective-permute-start(bf16[208,384]{1,0:T(8,128)(2,1)} %get-tuple-element.38), channel_id=1, source_target_pairs={{0,128},{64,192},{128,0},{192,64},{1,129},{65,193},{129,1},{193,65... | collective-permute-start | bytes 479240 | tf_op jit(solution)/shard_map/ppermute | solution.py:381
  13.2 1.0 copy-start.2
  14.2 0.9 copy-start.3
  26.7 12.3 %collective-permute-start.3 = (bf16[4,96,384]{2,1,0:T(8,128)(2,1)S(1)}, bf16[4,96,384]{2,1,0:T(8,128)(2,1)S(1)}, u32[]{:S(2)}, u32[]{:S(2)}) collective-permute-start(bf16[4,96,384]{2,1,0:T(8,128)(2,1)S(1)} %get-tuple-element.40.far_own.refs_0_), channel_id=1, source_target_pairs={{1,2},{3,4},{5,6},{7,8},{9,10},{11,12},{13,14},{15,16},{17,18},{19... | collective-permute-start | bytes 884744 | tf_op jit(solution)/shard_map/ppermute | solution.py:366
  28.6 10.3 %collective-permute-start.4 = (bf16[4,96,384]{2,1,0:T(8,128)(2,1)S(1)}, bf16[4,96,384]{2,1,0:T(8,128)(2,1)S(1)}, u32[]{:S(2)}, u32[]{:S(2)}) collective-permute-start(bf16[4,96,384]{2,1,0:T(8,128)(2,1)S(1)} %get-tuple-element.41.near_own.refs_1_), channel_id=1, source_target_pairs={{0,1},{2,3},{4,5},{6,7},{8,9},{10,11},{12,13},{14,15},{16,17},{18,... | collective-permute-start | bytes 884744 | tf_op jit(solution)/shard_map/ppermute | solution.py:366
  39.9 9.9 %collective-permute-start.5 = (bf16[96,384]{1,0:T(8,128)(2,1)S(1)}, bf16[96,384]{1,0:T(8,128)(2,1)S(1)}, u32[]{:S(2)}, u32[]{:S(2)}) collective-permute-start(bf16[96,384]{1,0:T(8,128)(2,1)S(1)} %get-tuple-element.45), channel_id=1, source_target_pairs={{1,2},{3,4},{5,6},{7,8},{9,10},{11,12},{13,14},{15,16},{17,18},{19... | collective-permute-start | bytes 221192 | tf_op jit(solution)/shard_map/ppermute | solution.py:366
  41.9 8.0 %collective-permute-start.6 = (bf16[96,384]{1,0:T(8,128)(2,1)S(1)}, bf16[96,384]{1,0:T(8,128)(2,1)S(1)}, u32[]{:S(2)}, u32[]{:S(2)}) collective-permute-start(bf16[96,384]{1,0:T(8,128)(2,1)S(1)} %get-tuple-element.46), channel_id=1, source_target_pairs={{0,1},{2,3},{4,5},{6,7},{8,9},{10,11},{12,13},{14,15},{16,17},{18,... | collective-permute-start | bytes 221192 | tf_op jit(solution)/shard_map/ppermute | solution.py:366
  50.6 9.9 %collective-permute-start.7 = (bf16[96,384]{1,0:T(8,128)(2,1)S(1)}, bf16[96,384]{1,0:T(8,128)(2,1)S(1)}, u32[]{:S(2)}, u32[]{:S(2)}) collective-permute-start(bf16[96,384]{1,0:T(8,128)(2,1)S(1)} %get-tuple-element.51), channel_id=1, source_target_pairs={{1,2},{3,4},{5,6},{7,8},{9,10},{11,12},{13,14},{15,16},{17,18},{19... | collective-permute-start | bytes 221192 | tf_op jit(solution)/shard_map/ppermute | solution.py:366
  52.5 8.0 %collective-permute-start.8 = (bf16[96,384]{1,0:T(8,128)(2,1)S(1)}, bf16[96,384]{1,0:T(8,128)(2,1)S(1)}, u32[]{:S(2)}, u32[]{:S(2)}) collective-permute-start(bf16[96,384]{1,0:T(8,128)(2,1)S(1)} %get-tuple-element.52), channel_id=1, source_target_pairs={{0,1},{2,3},{4,5},{6,7},{8,9},{10,11},{12,13},{14,15},{16,17},{18,... | collective-permute-start | bytes 221192 | tf_op jit(solution)/shard_map/ppermute | solution.py:366
  61.3 9.9 %collective-permute-start.9 = (bf16[96,384]{1,0:T(8,128)(2,1)S(1)}, bf16[96,384]{1,0:T(8,128)(2,1)S(1)}, u32[]{:S(2)}, u32[]{:S(2)}) collective-permute-start(bf16[96,384]{1,0:T(8,128)(2,1)S(1)} %get-tuple-element.55), channel_id=1, source_target_pairs={{1,2},{3,4},{5,6},{7,8},{9,10},{11,12},{13,14},{15,16},{17,18},{19... | collective-permute-start | bytes 221192 | tf_op jit(solution)/shard_map/ppermute | solution.py:366
  63.2 8.0 %collective-permute-start.10 = (bf16[96,384]{1,0:T(8,128)(2,1)S(1)}, bf16[96,384]{1,0:T(8,128)(2,1)S(1)}, u32[]{:S(2)}, u32[]{:S(2)}) collective-permute-start(bf16[96,384]{1,0:T(8,128)(2,1)S(1)} %get-tuple-element.56), channel_id=1, source_target_pairs={{0,1},{2,3},{4,5},{6,7},{8,9},{10,11},{12,13},{14,15},{16,17},{18,... | collective-permute-start | bytes 221192 | tf_op jit(solution)/shard_map/ppermute | solution.py:366
  72.4 13.7 %all-to-all-start = ((f32[16,4,384]{2,1,0:T(4,128)}), f32[16,4,384]{2,1,0:T(4,128)S(1)}, u32[]{:S(2)}, u32[]{:S(2)}) async-start(f32[16,4,384]{2,1,0:T(4,128)} %get-tuple-element.66), calls=%async_computation | async-start | bytes 196608 | tf_op jit(solution)/shard_map/all_to_all | solution.py:398
  76.1 10.0 %collective-permute-start.11 = (bf16[96,384]{1,0:T(8,128)(2,1)S(1)}, bf16[96,384]{1,0:T(8,128)(2,1)S(1)}, u32[]{:S(2)}, u32[]{:S(2)}) collective-permute-start(bf16[96,384]{1,0:T(8,128)(2,1)S(1)} %get-tuple-element.63), channel_id=1, source_target_pairs={{1,2},{3,4},{5,6},{7,8},{9,10},{11,12},{13,14},{15,16},{17,18},{19... | collective-permute-start | bytes 221192 | tf_op jit(solution)/shard_map/ppermute | solution.py:366
  81.7 4.5 %collective-permute-start.12 = (bf16[96,384]{1,0:T(8,128)(2,1)S(1)}, bf16[96,384]{1,0:T(8,128)(2,1)S(1)}, u32[]{:S(2)}, u32[]{:S(2)}) collective-permute-start(bf16[96,384]{1,0:T(8,128)(2,1)S(1)} %get-tuple-element.64), channel_id=1, source_target_pairs={{0,1},{2,3},{4,5},{6,7},{8,9},{10,11},{12,13},{14,15},{16,17},{18,... | collective-permute-start | bytes 221192 | tf_op jit(solution)/shard_map/ppermute | solution.py:366
  86.8 20.6 %all-to-all-start.1 = ((bf16[4,192,384]{2,1,0:T(8,128)(2,1)}), bf16[4,192,384]{2,1,0:T(8,128)(2,1)S(1)}, u32[]{:S(2)}, u32[]{:S(2)}) async-start(bf16[4,192,384]{2,1,0:T(8,128)(2,1)} %get-tuple-element.67), calls=%async_computation.1 | async-start | bytes 1179648 | tf_op jit(solution)/shard_map/all_to_all | solution.py:547
  92.5 5.0 %collective-permute-start.15 = (f32[1,4,1536]{2,1,0:T(4,128)S(1)}, f32[1,4,1536]{2,1,0:T(4,128)S(1)}, u32[]{:S(2)}, u32[]{:S(2)}) collective-permute-start(f32[1,4,1536]{2,1,0:T(4,128)S(1)} %get-tuple-element.68.own), channel_id=1, source_target_pairs={{0,6},{1,7},{2,4},{3,5},{4,2},{5,3},{6,0},{7,1},{8,14},{9,15},{10,... | collective-permute-start | bytes 73736 | tf_op jit(solution)/shard_map/ppermute | solution.py:408
  92.5 5.3 %collective-permute-start.14 = (f32[1,4,1536]{2,1,0:T(4,128)S(1)}, f32[1,4,1536]{2,1,0:T(4,128)S(1)}, u32[]{:S(2)}, u32[]{:S(2)}) collective-permute-start(f32[1,4,1536]{2,1,0:T(4,128)S(1)} %get-tuple-element.68.own), channel_id=1, source_target_pairs={{0,4},{1,5},{2,6},{3,7},{4,0},{5,1},{6,2},{7,3},{8,12},{9,13},{10,... | collective-permute-start | bytes 73736 | tf_op jit(solution)/shard_map/ppermute | solution.py:408
  92.5 6.1 %collective-permute-start.13 = (f32[1,4,1536]{2,1,0:T(4,128)S(1)}, f32[1,4,1536]{2,1,0:T(4,128)S(1)}, u32[]{:S(2)}, u32[]{:S(2)}) collective-permute-start(f32[1,4,1536]{2,1,0:T(4,128)S(1)} %get-tuple-element.68.own), channel_id=1, source_target_pairs={{0,2},{1,3},{2,0},{3,1},{4,6},{5,7},{6,4},{7,5},{8,10},{9,11},{10,... | collective-permute-start | bytes 73736 | tf_op jit(solution)/shard_map/ppermute | solution.py:408
  98.6 5.1 %collective-permute-start.18 = (f32[1,4,1536]{2,1,0:T(4,128)S(1)}, f32[1,4,1536]{2,1,0:T(4,128)S(1)}, u32[]{:S(2)}, u32[]{:S(2)}) collective-permute-start(f32[1,4,1536]{2,1,0:T(4,128)S(1)} %add_group.1.mods), channel_id=1, source_target_pairs={{0,24},{1,25},{2,26},{3,27},{4,28},{5,29},{6,30},{7,31},{8,16},{9,... | collective-permute-start | bytes 73736 | tf_op jit(solution)/shard_map/ppermute | solution.py:408
  98.7 5.4 %collective-permute-start.17 = (f32[1,4,1536]{2,1,0:T(4,128)S(1)}, f32[1,4,1536]{2,1,0:T(4,128)S(1)}, u32[]{:S(2)}, u32[]{:S(2)}) collective-permute-start(f32[1,4,1536]{2,1,0:T(4,128)S(1)} %add_group.1.mods), channel_id=1, source_target_pairs={{0,16},{1,17},{2,18},{3,19},{4,20},{5,21},{6,22},{7,23},{8,24},{9,... | collective-permute-start | bytes 73736 | tf_op jit(solution)/shard_map/ppermute | solution.py:408
  98.8 6.0 %collective-permute-start.16 = (f32[1,4,1536]{2,1,0:T(4,128)S(1)}, f32[1,4,1536]{2,1,0:T(4,128)S(1)}, u32[]{:S(2)}, u32[]{:S(2)}) collective-permute-start(f32[1,4,1536]{2,1,0:T(4,128)S(1)} %add_group.1.mods), channel_id=1, source_target_pairs={{0,8},{1,9},{2,10},{3,11},{4,12},{5,13},{6,14},{7,15},{8,0},{9,1},... | collective-permute-start | bytes 73736 | tf_op jit(solution)/shard_map/ppermute | solution.py:408
